TPU v7x, 128 devices: a whole 4x4x4 slice. The times are simulated.
128 devices in a mesh: user: 8 (over z, core), item: 16 (over x, y).
Axes of the slice: x: 4, y: 4, z: 4, core: 2. Of those that a mesh axis runs over, the one named last changes fastest.
Arguments:
- table: bfloat16 [65536, 512], P(('user', 'item')), may hold values from -6 to 6
- tower_first: bfloat16 [512, 512], replicated, may hold values from -0.25 to 0.25
- tower_second: bfloat16 [512, 512], replicated, may hold values from -0.25 to 0.25
- w_input: bfloat16 [512, 2048], replicated, may hold values from -0.25 to 0.25
- w_output: bfloat16 [512, 512], replicated, may hold values from -0.25 to 0.25
- norm_gain: float32 [512], replicated, may hold values from 0.1 to 1.9
- head_vec: float32 [512], replicated, may hold values from -0.25 to 0.25
- time_bias: float32 [4, 16], replicated, may hold values from -3 to 3
- look_owner: int32 [128, 768, 1], P(('user', 'item')), may hold values from 0 to 127; in each aligned block of 768 rows (0 to 767, 768 to 1535, ..., all dimensions but the last counted through in order) at most 12 rows name the same one
- look_row: int32 [128, 768], P(('user', 'item')), may hold values from 0 to 511
- event_time: int32 [128, 768], P(('user', 'item')), may hold values from 0 to 130624, as said below
- labels: int32 [128, 768], P(('user', 'item')), may hold values 0 or 1
Outputs:
- table_grad: float32 [65536, 512], P(('user', 'item'))
- tower_first_grad: float32 [512, 512], replicated
- tower_second_grad: float32 [512, 512], replicated
- input_grad: float32 [512, 2048], replicated
- output_grad: float32 [512, 512], replicated
- user_loss: float32 [128], P(('user', 'item'))
Inputs may be any that keep to these rules, and one draw needn't show every extreme that they name: `look_owner`: within one user's 768 lookups no owner is named more than 12 times; some owner is named exactly 12 times. `event_time`: history timestamps never fall; all candidates carry the request time, which is the largest value, later than every history event.
All inputs are finite; a program needn't handle non-finite values. No bound on the sum of `labels` on one device may be relied on, other than what follows from the above.
Results may differ from a plain program's by a relative error of at most 0.0095.
Values may be sent and summed in bfloat16 or wider, within the bound.
A program may use at most 128 MiB of HBM per device.

v0:
```python
import math

import jax
import jax.numpy as jnp
from jax import lax
from jax.sharding import PartitionSpec as P

HIST = 512


EPS = 1e-06


def tower_block(item_rows, first, second):
    hidden_items = jax.nn.silu(
        jnp.dot(item_rows.astype(jnp.bfloat16), first, preferred_element_type=jnp.float32)
    ).astype(jnp.bfloat16)
    return item_rows + jnp.dot(hidden_items, second, preferred_element_type=jnp.float32)


def user_loss_fn(token_rows, first, second, norm_gain, head_vec, time_bias, stamps, clicked):
    head_count, bucket_count = time_bias.shape
    positions, features = token_rows.shape
    head_size = features // head_count
    mean_sq = jnp.mean(token_rows * token_rows, axis=1, keepdims=True)
    normed = (token_rows * lax.rsqrt(mean_sq + EPS) * norm_gain).astype(jnp.bfloat16)
    proj = jax.nn.silu(jnp.dot(normed, first, preferred_element_type=jnp.float32)).astype(
        jnp.bfloat16
    )
    gates, values, queries, keys = jnp.split(proj, 4, axis=1)
    query_heads = queries.reshape(positions, head_count, head_size)
    key_heads = keys.reshape(positions, head_count, head_size)
    value_heads = values.reshape(positions, head_count, head_size)
    time_gap = stamps[:, None] - stamps[None, :HIST]
    time_term = jnp.zeros((head_count, positions, HIST), jnp.float32)
    for bucket in range(bucket_count):
        hit = (time_gap >= 2**bucket - 1).astype(jnp.float32)
        time_term = time_term + time_bias[:, bucket][:, None, None] * hit[None]
    score_scale = 1.0 / math.sqrt(head_size)
    scores = (
        jnp.einsum(
            "ihd,jhd->hij", query_heads, key_heads[:HIST], preferred_element_type=jnp.float32
        )
        * score_scale
        + time_term
    )
    allowed = jnp.arange(HIST)[None, :] <= jnp.arange(positions)[:, None]
    weights = (jnp.where(allowed[None], jax.nn.silu(scores), 0.0) / HIST).astype(jnp.bfloat16)
    attended = jnp.einsum(
        "hij,jhd->ihd", weights, value_heads[:HIST], preferred_element_type=jnp.float32
    )
    own_score = (
        jnp.sum(query_heads.astype(jnp.float32) * key_heads.astype(jnp.float32), axis=2)
        * score_scale
        + time_bias[:, 0][None, :]
    )
    is_cand = (jnp.arange(positions) >= HIST)[:, None]
    own_weight = (jnp.where(is_cand, jax.nn.silu(own_score), 0.0) / HIST).astype(jnp.bfloat16)
    attended = attended + own_weight.astype(jnp.float32)[:, :, None] * value_heads.astype(
        jnp.float32
    )
    attended = attended.reshape(positions, features)
    centered = attended - jnp.mean(attended, axis=1, keepdims=True)
    spread = lax.rsqrt(jnp.mean(centered * centered, axis=1, keepdims=True) + EPS)
    mixed_rows = (centered * spread * gates.astype(jnp.float32)).astype(jnp.bfloat16)
    output = token_rows + jnp.dot(mixed_rows, second, preferred_element_type=jnp.float32)
    logits = jnp.dot(output, head_vec, precision=lax.Precision.HIGHEST)
    return jnp.mean(jax.nn.softplus(logits) - clicked.astype(jnp.float32) * logits)


def body(
    table,
    tower_first,
    tower_second,
    w_input,
    w_output,
    norm_gain,
    head_vec,
    time_bias,
    look_owner,
    look_row,
    event_time,
    labels,
):
    n_user = lax.axis_size("user")
    n_item = lax.axis_size("item")
    owners = n_user * n_item
    lookups = look_row.shape[1]
    features = table.shape[1]
    capacity = max(2, 2 * lookups // owners)
    owner_ids = look_owner[0, :, 0]
    targets = jnp.arange(owners, dtype=jnp.int32)
    onehot = (owner_ids[:, None] == targets[None, :]).astype(jnp.int32)
    position = jnp.sum(onehot * (jnp.cumsum(onehot, axis=0) - 1), axis=1)
    slot_index = owner_ids * capacity + position
    send_ids = (
        jnp.full((owners * capacity,), -1, jnp.int32)
        .at[slot_index]
        .set(look_row[0])
        .reshape(owners, capacity)
    )
    recv_ids = lax.all_to_all(send_ids, ("user", "item"), split_axis=0, concat_axis=0, tiled=True)
    item_rows = table.astype(jnp.float32)
    embed_f, tower_back = jax.vjp(tower_block, item_rows, tower_first, tower_second)
    embedding = embed_f.astype(jnp.bfloat16)
    is_live = recv_ids >= 0
    safe_rows = jnp.where(is_live, recv_ids, 0)
    replies = jnp.where(is_live[:, :, None], embedding[safe_rows], jnp.zeros((), jnp.bfloat16))
    back_rows = lax.all_to_all(replies, ("user", "item"), split_axis=0, concat_axis=0, tiled=True)
    token_rows = back_rows.reshape(owners * capacity, features)[slot_index].astype(jnp.float32)

    def local_loss(rows_in, first, second):
        return user_loss_fn(
            rows_in, first, second, norm_gain, head_vec, time_bias, event_time[0], labels[0]
        )

    loss_value, hstu_back = jax.vjp(local_loss, token_rows, w_input, w_output)
    token_grad, input_term, output_term = hstu_back(jnp.ones((), jnp.float32))
    send_grad = (
        jnp.zeros((owners * capacity, features), jnp.float32)
        .at[slot_index]
        .set(token_grad)
        .reshape(owners, capacity, features)
    )
    recv_grad = lax.all_to_all(
        send_grad.astype(jnp.bfloat16), ("user", "item"), split_axis=0, concat_axis=0, tiled=True
    ).astype(send_grad.dtype)
    live_grad = jnp.where(is_live[:, :, None], recv_grad, 0.0).reshape(owners * capacity, features)
    embed_grad = jnp.zeros_like(item_rows).at[safe_rows.reshape(-1)].add(live_grad)
    table_grad, first_term, second_term = tower_back(embed_grad)
    input_grad, output_grad, first_grad, second_grad = lax.psum(
        (
            input_term.astype(jnp.float32),
            output_term.astype(jnp.float32),
            first_term.astype(jnp.float32),
            second_term.astype(jnp.float32),
        ),
        ("user", "item"),
    )
    return (table_grad, first_grad, second_grad, input_grad, output_grad, loss_value.reshape(1))


def solution(mesh):
    return jax.shard_map(
        body,
        mesh=mesh,
        in_specs=(
            P(("user", "item"), None),
            P(),
            P(),
            P(),
            P(),
            P(),
            P(),
            P(),
            P(("user", "item"), None, None),
            P(("user", "item"), None),
            P(("user", "item"), None),
            P(("user", "item"), None),
        ),
        out_specs=(P(("user", "item"), None), P(), P(), P(), P(), P(("user", "item"))),
        check_vma=False,
    )
```

profile of v0, /device:TPU:1, one launch (start us, length us, event | category | flops | bytes accessed | tf_op | source)
XLA Modules:
  0.0 440.2 jit_solution(1633673372559532998)
XLA Ops:
  13.1 11.5 %all-to-all-start = ((s32[128,1,12]{2,1,0:T(1,128)}), s32[128,1,12]{2,1,0:T(1,128)S(1)}, u32[]{:S(2)}, u32[]{:S(2)}) async-start(s32[128,1,12]{2,1,0:T(1,128)} %bitcast.4), calls=%async_computation | async-start | bytes 131072 | tf_op jit(solution)/shard_map/all_to_all | solution.py:102
  26.5 7.6 %all-to-all-done = s32[128,1,12]{2,1,0:T(1,128)S(1)} async-done(((s32[128,1,12]{2,1,0:T(1,128)}), s32[128,1,12]{2,1,0:T(1,128)S(1)}, u32[]{:S(2)}, u32[]{:S(2)}) %all-to-all-start) | async-done | bytes 6176 | tf_op jit(solution)/shard_map/all_to_all | solution.py:102
  34.2 5.4 %gather_fusion = bf16[1536,512]{1,0:T(8,128)(2,1)} fusion(bf16[512,512]{1,0:T(8,128)(2,1)S(1)} %fusion.54, s32[2048]{0:T(1024)S(1)} %pad_clamp_fusion), kind=kCustom, calls=%fused_computation | custom fusion | bytes 3151872 | tf_op jit(solution)/shard_map/gather | solution.py:108
  39.6 3.6 reshape.782
  46.3 6.0 %all-to-all-start.1 = ((bf16[128,12,512]{2,1,0:T(8,128)(2,1)}), bf16[128,12,512]{2,1,0:T(8,128)(2,1)}, u32[]{:S(2)}, u32[]{:S(2)}) async-start(bf16[128,12,512]{2,1,0:T(8,128)(2,1)} %broadcast_select_fusion), calls=%async_computation.1 | async-start | bytes 4194304 | tf_op jit(solution)/shard_map/all_to_all | solution.py:109
  54.2 8.7 %fusion.22 = (f32[768,512]{1,0:T(8,128)}, f32[768,512]{1,0:T(8,128)}, f32[768,512]{1,0:T(8,128)}, f32[768,512]{1,0:T(8,128)}, f32[768,512]{1,0:T(8,128)}, /*inde...) fusion(s32[512]{0:T(512)S(1)} %bitcast.96, ...), kind=kLoop, calls=%fused_computation.77 | loop fusion | flops 12976128 | bytes 25170944 | tf_op jit(solution)/shard_map/jvp()/convert_element_type | solution.py:37
  63.0 18.6 %all-to-all-done.1 = bf16[128,12,512]{2,1,0:T(8,128)(2,1)} async-done(((bf16[128,12,512]{2,1,0:T(8,128)(2,1)}), bf16[128,12,512]{2,1,0:T(8,128)(2,1)}, u32[]{:S(2)}, u32[]{:S(2)}) %all-to-all-start.1) | async-done | bytes 1572896 | tf_op jit(solution)/shard_map/all_to_all | solution.py:109
  81.6 3.7 reshape.770
  85.2 4.3 gather_fusion.1
  89.8 4.4 multiply_convert_fusion.1
  112.6 15.5 %multiply_convert_fusion = (bf16[4,768,512]{2,1,0:T(8,128)(2,1)S(1)}, f32[4,768,512]{2,1,0:T(8,128)}) fusion(pred[768,512]{1,0:T(8,128)(4,1)} %iota_compare_fusion, f32[768,512]{1,0:T(8,128)} %get-tuple-element.67, f32[4]{0:T(128)S(1)} %copy-done.48, f32[768,512]{1,0:T(8,128)} %get-tuple-element.68, f32[4]{0:T(128)S(1)} %copy-done.49, ...), kind=kOutput, calls=%fused_computation.30 | convolution fusion | flops 465567744 | bytes 36307200 | tf_op jit(solution)/shard_map/jvp(ihd,jhd->hij)/dot_general | solution.py:41
  152.5 4.0 fusion.62
  156.5 5.4 %fusion.4 = bf16[4,768,512]{2,1,0:T(8,128)(2,1)S(1)} fusion(f32[4,768,512]{2,1,0:T(8,128)} %get-tuple-element.85, pred[768,512]{1,0:T(8,128)(4,1)S(1)} %copy-done.26, f32[4,128,768]{1,0,2:T(4,128)S(1)} %bitcast.83, bf16[64,4,8,128]{3,2,1,0:T(8,128)(2,1)S(1)} %copy-done.18), kind=kOutput, calls=%fused_computation.29 | convolution fusion | flops 424673280 | bytes 11927552 | tf_op jit(solution)/shard_map/transpose(jvp(hij,jhd->ihd))/dot_general | solution.py:49
  171.5 4.4 fusion.45
  183.0 5.3 %fusion = bf16[768,2048]{1,0:T(8,128)(2,1)S(1)} fusion(f32[768,2048]{1,0:T(8,128)} %get-tuple-element.83, bf16[768,512]{1,0:T(8,128)(2,1)} %copy.145, bf16[768,512]{1,0:T(8,128)(2,1)} %copy.144, bf16[768,512]{1,0:T(8,128)(2,1)} %copy.143, bf16[768,512]{1,0:T(8,128)(2,1)} %get-tuple-element.63), kind=kLoop, calls=%fused_computation.25 | loop fusion | flops 28311552 | bytes 12582912 | tf_op jit(solution)/shard_map/transpose(jvp(jit(silu)))/add_any | solution.py:27
  191.1 8.6 %scatter_custom_fusion.1 = f32[1536,512]{1,0:T(8,128)} fusion(s32[768]{0:T(1024)S(1)} %fusion.105, bf16[768,512]{1,0:T(8,128)(2,1)S(1)} %gather_fusion.1, bf16[768,512]{1,0:T(8,128)(2,1)} %get-tuple-element.91, f32[]{:T(128)} %constant.30.clone.1, f32[768]{0:T(1024)S(1)} %multiply_multiply_fusion, f32[512]{0:T(512)S(1)} %copy-done.31, ...), kind=kCustom, calls=%fused_computation.60 | custom fusion | flops 3538944 | bytes 4734980 | tf_op jit(solution)/shard_map/scatter | solution.py:122
  206.5 5.5 %all-to-all-start.2 = ((bf16[128,12,512]{2,1,0:T(8,128)(2,1)}), bf16[128,12,512]{2,1,0:T(8,128)(2,1)}, u32[]{:S(2)}, u32[]{:S(2)}) async-start(bf16[128,12,512]{2,1,0:T(8,128)(2,1)} %convert_element_type.341), calls=%async_computation.2 | async-start | bytes 4194304 | tf_op jit(solution)/shard_map/all_to_all | solution.py:125
  216.3 5.8 %fusion.5 = f32[512,2048]{1,0:T(8,128)} fusion(bf16[768,2048]{1,0:T(8,128)(2,1)} %copy-done.4, bf16[768,512]{1,0:T(8,128)(2,1)S(1)} %gather_fusion.1, f32[512]{0:T(512)S(1)} %copy-done.27, f32[768]{0:T(1024)S(1)} %fusion.103), kind=kOutput, calls=%fused_computation.42 | convolution fusion | flops 1613234176 | bytes 8131584 | tf_op jit(solution)/shard_map/transpose(jvp())/dot_general | solution.py:27
  222.1 19.5 %all-to-all-done.2 = bf16[128,12,512]{2,1,0:T(8,128)(2,1)} async-done(((bf16[128,12,512]{2,1,0:T(8,128)(2,1)}), bf16[128,12,512]{2,1,0:T(8,128)(2,1)}, u32[]{:S(2)}, u32[]{:S(2)}) %all-to-all-start.2) | async-done | bytes 1572896 | tf_op jit(solution)/shard_map/all_to_all | solution.py:125
  241.6 3.7 convert_select_fusion
  245.3 4.7 %reshape.817 = f32[1536,512]{1,0:T(8,128)} reshape(f32[128,12,512]{2,1,0:T(8,128)} %convert_select_fusion) | data formatting | bytes 6291456 | tf_op jit(solution)/shard_map/reshape | solution.py:128
  249.9 10.5 %scatter_custom_fusion.2 = f32[512,512]{1,0:T(8,128)S(1)} fusion(s32[1536]{0:T(1024)S(1)} %fusion.95, f32[1536,512]{1,0:T(8,128)} %reshape.817, f32[]{:T(128)} %constant.30.clone.1), kind=kCustom, calls=%fused_computation.146 | custom fusion | flops 786432 | bytes 1049088 | tf_op jit(solution)/shard_map/scatter-add | solution.py:129
  268.8 153.8 %all-reduce.5.cloned.1.call-done = (f32[512,512]{0,1:T(8,128)}, f32[512,512]{1,0:T(8,128)}, f32[512,2048]{1,0:T(8,128)}, f32[512,512]{1,0:T(8,128)}) async-done(((f32[512,512]{0,1:T(8,128)}, f32[512,512]{1,0:T(8,128)}, f32[512,2048]{1,0:T(8,128)}, f32[512,512]{1,0:T(8,128)}), (f32[512,512]{0,1:T(8,128)}, f32[512,512]{1,0:T(8,128)}, f32[512,2048]{1,0:T(8,128)}, ...) | async-done | bytes 7340048 | tf_op jit(solution)/shard_map/psum | solution.py:131
  426.2 4.8 %copy.173 = f32[512,2048]{1,0:T(8,128)} copy(f32[512,2048]{1,0:T(8,128)} %get-tuple-element.95) | data formatting | bytes 8388608
  (185 shorter events, 98.3 us)
Async XLA Ops:
  7.2 82.6 %copy-start = (bf16[512,2048]{1,0:T(8,128)(2,1)S(1)}, bf16[512,2048]{1,0:T(8,128)(2,1)}, u32[]{:S(2)}) copy-start(bf16[512,2048]{1,0:T(8,128)(2,1)} %param.15) | copy-start | bytes 6291460
  8.2 16.4 %copy-start.13 = (bf16[512,512]{1,0:T(8,128)(2,1)S(1)}, bf16[512,512]{1,0:T(8,128)(2,1)}, u32[]{:S(2)}) copy-start(bf16[512,512]{1,0:T(8,128)(2,1)} %param.12) | copy-start | bytes 1572868
  8.5 16.1 %copy-start.15 = (bf16[512,512]{1,0:T(8,128)(2,1)S(1)}, bf16[512,512]{1,0:T(8,128)(2,1)}, u32[]{:S(2)}) copy-start(bf16[512,512]{1,0:T(8,128)(2,1)} %param.13) | copy-start | bytes 1572868
  13.1 21.0 %all-to-all-start = ((s32[128,1,12]{2,1,0:T(1,128)}), s32[128,1,12]{2,1,0:T(1,128)S(1)}, u32[]{:S(2)}, u32[]{:S(2)}) async-start(s32[128,1,12]{2,1,0:T(1,128)} %bitcast.4), calls=%async_computation | async-start | bytes 131072 | tf_op jit(solution)/shard_map/all_to_all | solution.py:102
  46.2 6.0 %copy-start.29 = (s32[1,768]{1,0:T(1,128)S(1)}, s32[1,768]{1,0:T(1,128)}, u32[]{:S(2)}) copy-start(s32[1,768]{1,0:T(1,128)} %param.22) | copy-start | bytes 9220
  46.2 6.1 %copy-start.34 = (s32[1,768]{1,0:T(1,128)S(1)}, s32[1,768]{1,0:T(1,128)}, u32[]{:S(2)}) copy-start(s32[1,768]{1,0:T(1,128)} %param.23) | copy-start | bytes 9220
  46.2 6.1 %copy-start.24 = (f32[4,16]{1,0:T(4,128)S(1)}, f32[4,16]{1,0:T(4,128)}, u32[]{:S(2)}) copy-start(f32[4,16]{1,0:T(4,128)} %param.19) | copy-start | bytes 772
  46.2 8.0 %slice-start = ((s32[1,768]{1,0:T(1,128)}), s32[1,512]{1,0:T(1,128)S(1)}, s32[]{:S(2)}) async-start(s32[1,768]{1,0:T(1,128)} %param.22), calls=%async_computation.4 | async-start | bytes 4096 | tf_op jit(solution)/shard_map/jvp()/slice | solution.py:34
  46.3 35.3 %all-to-all-start.1 = ((bf16[128,12,512]{2,1,0:T(8,128)(2,1)}), bf16[128,12,512]{2,1,0:T(8,128)(2,1)}, u32[]{:S(2)}, u32[]{:S(2)}) async-start(bf16[128,12,512]{2,1,0:T(8,128)(2,1)} %broadcast_select_fusion), calls=%async_computation.1 | async-start | bytes 4194304 | tf_op jit(solution)/shard_map/all_to_all | solution.py:109
  52.3 60.0 %copy-start.33 = (pred[768]{0:T(1024)(128)(4,1)}, pred[768]{0:T(1024)(128)(4,1)S(1)}, u32[]{:S(2)}) copy-start(pred[768]{0:T(1024)(128)(4,1)S(1)} %iota_compare_fusion.4) | copy-start | bytes 2308
  53.4 59.0 %copy-start.32 = (f32[4]{0:T(128)}, f32[4]{0:T(128)S(1)}, u32[]{:S(2)}) copy-start(f32[4]{0:T(128)S(1)} %get-tuple-element.36) | copy-start | bytes 52
  85.2 4.6 %copy-start.27 = (f32[512]{0:T(512)S(1)}, f32[512]{0:T(512)}, u32[]{:S(2)}) copy-start(f32[512]{0:T(512)} %param.17) | copy-start | bytes 6148
  94.2 2.9 copy-start.8
  112.6 15.5 %copy-start.10 = (f32[768,4,128]{0,2,1:T(8,128)S(1)}, f32[768,4,128]{0,2,1:T(8,128)}, u32[]{:S(2)}) copy-start(f32[768,4,128]{0,2,1:T(8,128)} %copy.124) | copy-start | bytes 4718596
  112.6 15.5 %copy-start.17 = (bf16[64,4,8,128]{3,2,1,0:T(8,128)(2,1)S(1)}, bf16[64,4,8,128]{3,2,1,0:T(8,128)(2,1)}, u32[]{:S(2)}) copy-start(bf16[64,4,8,128]{3,2,1,0:T(8,128)(2,1)} %get-tuple-element.58) | copy-start | bytes 1572868
  137.0 2.8 copy-start.9
  152.5 4.0 copy-start.1
  152.5 4.0 copy-start.18
  152.5 4.0 copy-start.26
  156.5 7.1 %copy-start.7 = (bf16[768,512]{0,1:T(8,128)(2,1)S(1)}, bf16[768,512]{0,1:T(8,128)(2,1)}, u32[]{:S(2)}) copy-start(bf16[768,512]{0,1:T(8,128)(2,1)} %copy.147) | copy-start | bytes 2359300
  188.3 2.8 copy-start.31
  206.5 35.1 %all-to-all-start.2 = ((bf16[128,12,512]{2,1,0:T(8,128)(2,1)}), bf16[128,12,512]{2,1,0:T(8,128)(2,1)}, u32[]{:S(2)}, u32[]{:S(2)}) async-start(bf16[128,12,512]{2,1,0:T(8,128)(2,1)} %convert_element_type.341), calls=%async_computation.2 | async-start | bytes 4194304 | tf_op jit(solution)/shard_map/all_to_all | solution.py:125
  212.0 210.6 %all-reduce.5.cloned.1.call-start = ((), (), s32[]{:S(2)}) async-start(), calls=%async_computation.3 | async-start | bytes 14680064 | tf_op jit(solution)/shard_map/psum | solution.py:131
  426.2 4.8 %copy-start.22 = (f32[512,512]{1,0:T(8,128)S(1)}, f32[512,512]{1,0:T(8,128)}, u32[]{:S(2)}) copy-start(f32[512,512]{1,0:T(8,128)} %get-tuple-element.96) | copy-start | bytes 3145732
  (32 other events, 67.9 us)
Sparse Core Ops, SparseCore 0:
  265.7 156.9 all-reduce.4
where the time goes:
time: 446 us; the launch traced here: 440 us
  waiting for transfers between devices  200 us (45%)
  local copies, waits for them, and re-layouts  74.1 us (17%)
  other arithmetic  66.7 us (15%)
  matrix products  60 us (13%)
  starting transfers between devices  23 us (5%)
  between operations  16.8 us (4%)
    psum x1, waiting for transfers between devices, body(): lax.psum((input_term.astype(jnp.float32), output_term.astype(jnp.float32)...  154 us
    dot_general x3, matrix products, user_loss_fn(): jnp.einsum('ihd,jhd->hij', query_heads, key_heads[:HIST], preferred_eleme...  21.2 us
    all_to_all x1, waiting for transfers between devices, body(): lax.all_to_all(send_grad.astype(jnp.bfloat16), ('user', 'item'), split_ax...  19.5 us
    all_to_all x1, waiting for transfers between devices, body(): lax.all_to_all(replies, ('user', 'item'), split_axis=0, concat_axis=0, ti...  18.6 us
    unnamed x107, local copies, waits for them, and re-layouts  14.2 us
    dot_general x3, matrix products, user_loss_fn(): jnp.dot(normed, first, preferred_element_type=jnp.float32)  12.9 us
    dot_general x3, matrix products, user_loss_fn(): jnp.einsum('hij,jhd->ihd', weights, value_heads[:HIST], preferred_element...  11.8 us
    all_to_all x1, starting transfers between devices, body(): lax.all_to_all(send_ids, ('user', 'item'), split_axis=0, concat_axis=0, t...  11.5 us
  transfers between devices with their start and end apart: 4, of which 4 were waited for; matrix products, arithmetic and copies ran while one was open for 5% of the time, Pallas kernels for 0%

commit v1 on v0

v1 whole, which is shorter than its diff:
```python
import math

import jax
import jax.numpy as jnp
from jax import lax
from jax.experimental import pallas as pl
from jax.experimental.pallas import tpu as pltpu
from jax.sharding import PartitionSpec as P

D = 512
HEADS = 4
HD = 128
HIST = 512
LOOK = 768
BUCKETS = 16
EPS = 1e-06
F32 = jnp.float32
BF16 = jnp.bfloat16
RB = 128
NEG = -1e30


def nn(a, b):
    return lax.dot_general(a, b, (((1,), (0,)), ((), ())), preferred_element_type=F32)


def nt(a, b):
    return lax.dot_general(a, b, (((1,), (1,)), ((), ())), preferred_element_type=F32)


def sigmoid(x):
    return 0.5 + 0.5 * jnp.tanh(0.5 * x)


def keys_of(start):
    return min(HIST, start + RB)


def hstu_kernel(
    tok_ref, w1_ref, w2_ref, gain_ref, head_ref, tb_ref, stamp_row_ref, stamp_col_ref, label_ref,
    tgrad_ref, iterm_ref, uvec_ref, loss_ref,
    normed, proj, dsl, idx, wts, dwt, att, dp, dkv,
):
    gain = gain_ref[...]
    head = head_ref[...]
    scale = 1.0 / math.sqrt(HD)
    for s in range(0, LOOK, RB):
        rows = pl.ds(s, RB)
        t = tok_ref[rows, :].astype(F32)
        r = lax.rsqrt(jnp.mean(t * t, axis=1, keepdims=True) + EPS)
        normed[rows, :] = (t * r * gain).astype(BF16)
    for c in range(0, 4 * D, 256):
        cols = pl.ds(c, 256)
        for s in range(0, LOOK, RB):
            rows = pl.ds(s, RB)
            p = nn(normed[rows, :], w1_ref[:, cols])
            sg = sigmoid(p)
            y = p * sg
            proj[rows, cols] = y.astype(BF16)
            dsl[rows, cols] = (sg + y * (1.0 - sg)).astype(BF16)
    lane = lax.broadcasted_iota(jnp.int32, (HEADS, 128), 1)
    tab = jnp.zeros((HEADS, 128), F32)
    for k in range(BUCKETS):
        tab = tab + jnp.where(lane <= 31 - k, tb_ref[:, k : k + 1], 0.0)
    tab = jnp.where(lane == 33, NEG, tab)
    for s in range(0, LOOK, RB):
        rows = pl.ds(s, RB)
        ke = keys_of(s)
        gap = stamp_col_ref[rows, :] - stamp_row_ref[:, 0:ke]
        lz = lax.clz(gap + 1)
        if s < HIST:
            i_pos = s + lax.broadcasted_iota(jnp.int32, (RB, ke), 0)
            j_pos = lax.broadcasted_iota(jnp.int32, (RB, ke), 1)
            lz = jnp.where(j_pos <= i_pos, lz, 33)
        idx[rows, 0:ke] = lz
    for h in range(HEADS):
        hc = h * HD
        tab_h = jnp.broadcast_to(tab[h : h + 1, :], (RB, 128))
        for s in range(0, LOOK, RB):
            rows = pl.ds(s, RB)
            ke = keys_of(s)
            q = proj[rows, pl.ds(2 * D + hc, HD)]
            sc = nt(q, proj[0:ke, pl.ds(3 * D + hc, HD)]) * scale
            tt = [
                jnp.take_along_axis(tab_h, idx[rows, j : j + 128], axis=1)
                for j in range(0, ke, 128)
            ]
            sc = sc + jnp.concatenate(tt, axis=1)
            sg = sigmoid(sc)
            y = sc * sg
            w = (y * (1.0 / HIST)).astype(BF16)
            wts[h, rows, 0:ke] = w
            dwt[h, rows, 0:ke] = ((sg + y * (1.0 - sg)) * (1.0 / HIST)).astype(BF16)
            if ke < HIST:
                wts[h, rows, ke:HIST] = jnp.zeros((RB, HIST - ke), BF16)
            att[rows, pl.ds(hc, HD)] = nn(w, proj[0:ke, pl.ds(D + hc, HD)])
    own = {}
    for h in range(HEADS):
        hc = h * HD
        for s in range(HIST, LOOK, RB):
            rows = pl.ds(s, RB)
            q = proj[rows, pl.ds(2 * D + hc, HD)].astype(F32)
            k = proj[rows, pl.ds(3 * D + hc, HD)].astype(F32)
            v = proj[rows, pl.ds(D + hc, HD)].astype(F32)
            os = jnp.sum(q * k, axis=1, keepdims=True) * scale + tb_ref[h : h + 1, 0:1]
            sg = sigmoid(os)
            y = os * sg
            ow = (y * (1.0 / HIST)).astype(BF16).astype(F32)
            own[h, s] = (ow, (sg + y * (1.0 - sg)) * (1.0 / HIST))
            att[rows, pl.ds(hc, HD)] += ow * v
    h_hi = head.astype(BF16)
    h_mid = (head - h_hi.astype(F32)).astype(BF16)
    h_lo = (head - h_hi.astype(F32) - h_mid.astype(F32)).astype(BF16)
    parts = jnp.concatenate([h_hi, h_mid, h_lo, jnp.zeros((13, D), BF16)], axis=0)
    hw = jnp.sum(nt(parts, w2_ref[...]), axis=0, keepdims=True)
    loss = jnp.zeros((1, 1), F32)
    uvec = jnp.zeros((1, D), F32)
    dlogit = {}
    for s in range(0, LOOK, RB):
        rows = pl.ds(s, RB)
        a = att[rows, :]
        cen = a - jnp.mean(a, axis=1, keepdims=True)
        spread = lax.rsqrt(jnp.mean(cen * cen, axis=1, keepdims=True) + EPS)
        n = cen * spread
        g = proj[rows, 0:D].astype(F32)
        mixed = (n * g).astype(BF16).astype(F32)
        t = tok_ref[rows, :].astype(F32)
        logit = jnp.sum(t * head + mixed * hw, axis=1, keepdims=True)
        lab = label_ref[rows, :].astype(F32)
        soft = jnp.maximum(logit, 0.0) + jnp.log1p(jnp.exp(-jnp.abs(logit)))
        loss = loss + jnp.sum(soft - lab * logit, axis=0, keepdims=True)
        dl = (jax.nn.sigmoid(logit) - lab) * (1.0 / LOOK)
        dlogit[s] = dl
        uvec = uvec + jnp.sum(mixed * dl, axis=0, keepdims=True)
        dm = (dl * hw).astype(BF16).astype(F32)
        dg = dm * n
        dp[rows, 0:D] = (dg * dsl[rows, 0:D].astype(F32)).astype(BF16)
        dn = dm * g
        da = spread * (
            dn - jnp.mean(dn, axis=1, keepdims=True) - n * jnp.mean(dn * n, axis=1, keepdims=True)
        )
        att[rows, :] = da
    uvec_ref[...] = uvec
    loss_ref[...] = jnp.broadcast_to(loss * (1.0 / LOOK), loss_ref.shape)
    for h in range(HEADS):
        hc = h * HD
        for s in range(0, LOOK, RB):
            rows = pl.ds(s, RB)
            ke = keys_of(s)
            da = att[rows, pl.ds(hc, HD)]
            dw = nt(da.astype(BF16), proj[0:ke, pl.ds(D + hc, HD)])
            ds = (dw * dwt[h, rows, 0:ke].astype(F32) * scale).astype(BF16)
            dwt[h, rows, 0:ke] = ds
            if ke < HIST:
                dwt[h, rows, ke:HIST] = jnp.zeros((RB, HIST - ke), BF16)
            dq = nn(ds, proj[0:ke, pl.ds(3 * D + hc, HD)])
            if s >= HIST:
                q = proj[rows, pl.ds(2 * D + hc, HD)].astype(F32)
                k = proj[rows, pl.ds(3 * D + hc, HD)].astype(F32)
                v = proj[rows, pl.ds(D + hc, HD)].astype(F32)
                ow, osl = own[h, s]
                dos = jnp.sum(da * v, axis=1, keepdims=True) * osl * scale
                dq = dq + dos * k
                dcol = pl.ds(D + hc, HD)
                dp[rows, dcol] = (ow * da * dsl[rows, dcol].astype(F32)).astype(BF16)
                dcol = pl.ds(3 * D + hc, HD)
                dp[rows, dcol] = (dos * q * dsl[rows, dcol].astype(F32)).astype(BF16)
            dcol = pl.ds(2 * D + hc, HD)
            dp[rows, dcol] = (dq * dsl[rows, dcol].astype(F32)).astype(BF16)
        hist = pl.ds(0, HIST)
        dat = att[:, pl.ds(hc, HD)].T.astype(BF16)
        dcol = pl.ds(D + hc, HD)
        dp[hist, dcol] = (nn(dat, wts[h]).T * dsl[hist, dcol].astype(F32)).astype(BF16)
        qt = proj[:, pl.ds(2 * D + hc, HD)].astype(F32).T.astype(BF16)
        dcol = pl.ds(3 * D + hc, HD)
        dp[hist, dcol] = (nn(qt, dwt[h]).T * dsl[hist, dcol].astype(F32)).astype(BF16)
    for s in range(0, LOOK, RB):
        rows = pl.ds(s, RB)
        dnorm = nt(dp[rows, :], w1_ref[...])
        t = tok_ref[rows, :].astype(F32)
        r = lax.rsqrt(jnp.mean(t * t, axis=1, keepdims=True) + EPS)
        tn = dnorm * gain
        tgrad_ref[rows, :] = (
            dlogit[s] * head + r * tn - t * (r * r * r * jnp.mean(tn * t, axis=1, keepdims=True))
        ).astype(BF16)
    nrt = normed[...].astype(F32).T.astype(BF16)
    for c in range(0, 4 * D, 256):
        cols = pl.ds(c, 256)
        iterm_ref[:, cols] = nn(nrt, dp[:, cols]).astype(BF16)


def hstu(tok, w1, w2, gain, head, tb, stamps, labels):
    vm = pl.BlockSpec(memory_space=pltpu.VMEM)
    return pl.pallas_call(
        hstu_kernel,
        out_shape=(
            jax.ShapeDtypeStruct((LOOK, D), BF16),
            jax.ShapeDtypeStruct((D, 4 * D), BF16),
            jax.ShapeDtypeStruct((1, D), F32),
            jax.ShapeDtypeStruct((1, 128), F32),
        ),
        in_specs=[vm] * 9,
        out_specs=(vm,) * 4,
        scratch_shapes=[
            pltpu.VMEM((LOOK, D), BF16),
            pltpu.VMEM((LOOK, 4 * D), BF16),
            pltpu.VMEM((LOOK, 4 * D), BF16),
            pltpu.VMEM((LOOK, HIST), jnp.int32),
            pltpu.VMEM((HEADS, LOOK, HIST), BF16),
            pltpu.VMEM((HEADS, LOOK, HIST), BF16),
            pltpu.VMEM((LOOK, D), F32),
            pltpu.VMEM((LOOK, 4 * D), BF16),
            pltpu.VMEM((8, 128), F32),
        ],
        compiler_params=pltpu.CompilerParams(vmem_limit_bytes=56 * 2**20),
        cost_estimate=pl.CostEstimate(flops=8 * 10**9, bytes_accessed=8 * 2**20, transcendentals=4 * 10**6),
        name="hstu",
    )(
        tok, w1, w2, gain.reshape(1, D), head.reshape(1, D), tb,
        stamps.reshape(1, LOOK), stamps.reshape(LOOK, 1), labels.reshape(LOOK, 1),
    )


def tower_block(item_rows, first, second):
    hidden_items = jax.nn.silu(
        jnp.dot(item_rows.astype(jnp.bfloat16), first, preferred_element_type=jnp.float32)
    ).astype(jnp.bfloat16)
    return item_rows + jnp.dot(hidden_items, second, preferred_element_type=jnp.float32)


def body(
    table, tower_first, tower_second, w_input, w_output, norm_gain, head_vec, time_bias,
    look_owner, look_row, event_time, labels,
):
    n_user = lax.axis_size("user")
    n_item = lax.axis_size("item")
    owners = n_user * n_item
    lookups = look_row.shape[1]
    features = table.shape[1]
    capacity = 12
    owner_ids = look_owner[0, :, 0]
    targets = jnp.arange(owners, dtype=jnp.int32)
    onehot = (owner_ids[:, None] == targets[None, :]).astype(jnp.int32)
    position = jnp.sum(onehot * (jnp.cumsum(onehot, axis=0) - 1), axis=1)
    slot_index = owner_ids * capacity + position
    send_ids = (
        jnp.full((owners * capacity,), -1, jnp.int32)
        .at[slot_index]
        .set(look_row[0])
        .reshape(owners, capacity)
    )
    recv_ids = lax.all_to_all(send_ids, ("user", "item"), split_axis=0, concat_axis=0, tiled=True)
    item_rows = table.astype(jnp.float32)
    embed_f, tower_back = jax.vjp(tower_block, item_rows, tower_first, tower_second)
    embedding = embed_f.astype(jnp.bfloat16)
    is_live = recv_ids >= 0
    safe_rows = jnp.where(is_live, recv_ids, 0)
    replies = jnp.where(is_live[:, :, None], embedding[safe_rows], jnp.zeros((), jnp.bfloat16))
    back_rows = lax.all_to_all(replies, ("user", "item"), split_axis=0, concat_axis=0, tiled=True)
    tok = back_rows.reshape(owners * capacity, features)[slot_index]
    token_grad, input_term, uvec, loss = hstu(
        tok, w_input, w_output, norm_gain, head_vec, time_bias, event_time, labels
    )
    send_grad = (
        jnp.zeros((owners * capacity, features), BF16)
        .at[slot_index]
        .set(token_grad)
        .reshape(owners, capacity, features)
    )
    input_grad, uvec = lax.psum((input_term.astype(F32), uvec[0]), ("user", "item"))
    output_grad = uvec[:, None] * head_vec[None, :]
    recv_grad = lax.all_to_all(
        send_grad, ("user", "item"), split_axis=0, concat_axis=0, tiled=True
    ).astype(F32)
    live_grad = jnp.where(is_live[:, :, None], recv_grad, 0.0).reshape(owners * capacity, features)
    embed_grad = jnp.zeros_like(item_rows).at[safe_rows.reshape(-1)].add(live_grad)
    table_grad, first_term, second_term = tower_back(embed_grad)
    first_grad, second_grad = lax.psum(
        (first_term.astype(F32), second_term.astype(F32)), ("user", "item")
    )
    return (table_grad, first_grad, second_grad, input_grad, output_grad, loss[0, :1])


def solution(mesh):
    return jax.shard_map(
        body,
        mesh=mesh,
        in_specs=(
            P(("user", "item"), None), P(), P(), P(), P(), P(), P(), P(),
            P(("user", "item"), None, None), P(("user", "item"), None),
            P(("user", "item"), None), P(("user", "item"), None),
        ),
        out_specs=(P(("user", "item"), None), P(), P(), P(), P(), P(("user", "item"))),
        check_vma=False,
    )
```

time: 446 us -> 337 us (0.76)
  blocking collectives: 0 us -> 104 us
  waiting for transfers between devices: 200 us -> 105 us
  matrix products: 60 us -> 7.21 us
  other arithmetic: 66.7 us -> 19.8 us
  local copies, waits for them, and re-layouts: 74.1 us -> 36.5 us
  Pallas kernels: 0 us -> 23.2 us
    psum x1, waiting for transfers between devices: 154 us -> 41.3 us  [body(): lax.psum((first_term.astype(F32), second_term.astype(F32)), ('user', 'ite...]
    psum x0 -> x1, blocking collectives: none -> 104 us  [body(): lax.psum((input_term.astype(F32), uvec[0]), ('user', 'item'))]
    dot_general x13 -> x0, matrix products: 51.5 us -> none  [the longest x3 21.2 us: user_loss_fn(): jnp.einsum('ihd,jhd->hij', query_heads, key_heads[:HIST], preferred_eleme...]
    pallas_call x0 -> x1, Pallas kernels: none -> 23.2 us  [hstu(): pl.pallas_call(hstu_kernel, out_shape=(jax.ShapeDtypeStruct((LOOK, D), BF...]
    convert_element_type x6 -> x0, other arithmetic: 15.9 us -> none  [the longest x1 8.72 us: user_loss_fn(): hit = (time_gap >= 2 ** bucket - 1).astype(jnp.float32)]
    reshape x8 -> x4, local copies, waits for them, and re-layouts: 21.3 us -> 5.87 us  [the longest x1 2.47 us: body(): tok = back_rows.reshape(owners * capacity, features)[slot_index]]
    convert_element_type x4 -> x0, local copies, waits for them, and re-layouts: 12.1 us -> none  [the longest x2 5.4 us: user_loss_fn(): value_heads.astype(jnp.float32)]
    add_any x4 -> x0, other arithmetic: 11.4 us -> none  [the longest x1 5.3 us: user_loss_fn(): jax.nn.silu(jnp.dot(normed, first, preferred_element_type=jnp.float32))]
  transfers between devices with their start and end apart: 4 -> 4, of which waited for: 4 -> 4; matrix products, arithmetic and copies ran while one was open for 5% -> 2% of each run, Pallas kernels for 0% -> 0%
where the time goes in v1:
time: 337 us; the launch traced here: 332 us
  waiting for transfers between devices  105 us (31%)
  blocking collectives  104 us (31%)
  local copies, waits for them, and re-layouts  36.5 us (11%)
  Pallas kernels  23.2 us (7%)
  starting transfers between devices  21.6 us (6%)
  other arithmetic  19.8 us (6%)
  between operations  14.6 us (4%)
  matrix products  7.21 us (2%)
    psum x1, blocking collectives, body(): lax.psum((input_term.astype(F32), uvec[0]), ('user', 'item'))  104 us
    psum x1, waiting for transfers between devices, body(): lax.psum((first_term.astype(F32), second_term.astype(F32)), ('user', 'ite...  41.3 us
    all_to_all x1, waiting for transfers between devices, body(): lax.all_to_all(send_grad, ('user', 'item'), split_axis=0, concat_axis=0,...  28.3 us
    all_to_all x1, waiting for transfers between devices, body(): lax.all_to_all(replies, ('user', 'item'), split_axis=0, concat_axis=0, ti...  27.6 us
    pallas_call x1, Pallas kernels, hstu(): pl.pallas_call(hstu_kernel, out_shape=(jax.ShapeDtypeStruct((LOOK, D), BF...  23.2 us
    all_to_all x1, starting transfers between devices, body(): lax.all_to_all(send_ids, ('user', 'item'), split_axis=0, concat_axis=0, t...  11.5 us
    scatter-add x1, other arithmetic, body(): jnp.zeros_like(item_rows).at[safe_rows.reshape(-1)].add(live_grad)  10.5 us
    all_to_all x1, waiting for transfers between devices, body(): lax.all_to_all(send_ids, ('user', 'item'), split_axis=0, concat_axis=0, t...  8.06 us
  transfers between devices with their start and end apart: 4, of which 4 were waited for; matrix products, arithmetic and copies ran while one was open for 2% of the time, Pallas kernels for 0%

profile of v1, /device:TPU:1, one launch (start us, length us, event | category | flops | bytes accessed | tf_op | source)
XLA Modules:
  0.0 331.8 jit_solution(18331153896462863300)
XLA Ops:
  9.6 3.4 %scatter_custom_fusion = s32[1536]{0:T(1024)S(1)} fusion(s32[768]{0:T(1024)S(1)} %fusion.19, s32[768]{0:T(1024)S(1)} %reduce.3, s32[]{:T(128)} %constant.9.clone.1), kind=kCustom, calls=%fused_computation.48 | custom fusion | bytes 6148 | tf_op jit(solution)/shard_map/scatter | solution.py:249
  13.7 11.5 %all-to-all-start = ((s32[128,1,12]{2,1,0:T(1,128)}), s32[128,1,12]{2,1,0:T(1,128)S(1)}, u32[]{:S(2)}, u32[]{:S(2)}) async-start(s32[128,1,12]{2,1,0:T(1,128)} %bitcast.4), calls=%async_computation | async-start | bytes 131072 | tf_op jit(solution)/shard_map/all_to_all | solution.py:252
  26.6 8.1 %all-to-all-done = s32[128,1,12]{2,1,0:T(1,128)S(1)} async-done(((s32[128,1,12]{2,1,0:T(1,128)}), s32[128,1,12]{2,1,0:T(1,128)S(1)}, u32[]{:S(2)}, u32[]{:S(2)}) %all-to-all-start) | async-done | bytes 6176 | tf_op jit(solution)/shard_map/all_to_all | solution.py:252
  35.1 4.8 %gather_fusion = bf16[1536,512]{1,0:T(8,128)(2,1)S(1)} fusion(bf16[512,512]{1,0:T(8,128)(2,1)S(1)} %fusion.5, s32[2048]{0:T(1024)S(1)} %pad_clamp_fusion), kind=kCustom, calls=%fused_computation | custom fusion | bytes 3151872 | tf_op jit(solution)/shard_map/gather | solution.py:258
  39.9 1.5 reshape.158
  41.4 2.7 broadcast_select_fusion
  44.1 5.6 %all-to-all-start.1 = ((bf16[128,12,512]{2,1,0:T(8,128)(2,1)}), bf16[128,12,512]{2,1,0:T(8,128)(2,1)}, u32[]{:S(2)}, u32[]{:S(2)}) async-start(bf16[128,12,512]{2,1,0:T(8,128)(2,1)} %broadcast_select_fusion), calls=%async_computation.1 | async-start | bytes 4194304 | tf_op jit(solution)/shard_map/all_to_all | solution.py:259
  51.7 27.6 %all-to-all-done.1 = bf16[128,12,512]{2,1,0:T(8,128)(2,1)} async-done(((bf16[128,12,512]{2,1,0:T(8,128)(2,1)}), bf16[128,12,512]{2,1,0:T(8,128)(2,1)}, u32[]{:S(2)}, u32[]{:S(2)}) %all-to-all-start.1) | async-done | bytes 1572896 | tf_op jit(solution)/shard_map/all_to_all | solution.py:259
  79.3 2.5 reshape.150
  81.8 3.8 %gather_fusion.1 = bf16[768,512]{1,0:T(8,128)(2,1)} fusion(bf16[1536,512]{1,0:T(8,128)(2,1)S(1)} %reshape.150, s32[1024]{0:T(1024)S(1)} %pad_clamp_fusion.1), kind=kCustom, calls=%fused_computation.1 | custom fusion | bytes 1575936 | tf_op jit(solution)/shard_map/gather | solution.py:260
  85.5 23.2 %hstu.1 = (bf16[768,512]{1,0:T(8,128)(2,1)}, bf16[512,2048]{1,0:T(8,128)(2,1)}, f32[1,512]{1,0:T(1,128)}, f32[1,128]{1,0:T(1,128)}) custom-call(bf16[768,512]{1,0:T(8,128)(2,1)} %gather_fusion.1, bf16[512,2048]{1,0:T(8,128)(2,1)} %w1_ref.1, bf16[512,512]{1,0:T(8,128)(2,1)} %w2_ref.1, f32[1,512]{1,0:T(1,128)} %bitcast.48, f32[1,512]{1,0:T(1,128)} %bitcast.46, ...), custom_call_target="tpu_custom_call" | custom-call | flops 8000000000 | bytes 8388608 | tf_op jit(solution)/shard_map/hstu/pallas_call | solution.py:194
  108.7 6.5 %scatter_custom_fusion.1 = bf16[1536,512]{1,0:T(8,128)(2,1)S(1)} fusion(s32[768]{0:T(1024)S(1)} %fusion.19, bf16[768,512]{1,0:T(8,128)(2,1)} %get-tuple-element.10, bf16[]{:T(256)} %constant.14.clone.1), kind=kCustom, calls=%fused_computation.25 | custom fusion | bytes 1573376 | tf_op jit(solution)/shard_map/scatter | solution.py:267
  115.2 1.5 reshape.155
  116.8 4.5 %all-to-all-start.2 = ((bf16[128,12,512]{2,1,0:T(8,128)(2,1)}), bf16[128,12,512]{2,1,0:T(8,128)(2,1)S(1)}, u32[]{:S(2)}, u32[]{:S(2)}) async-start(bf16[128,12,512]{2,1,0:T(8,128)(2,1)} %reshape.155), calls=%async_computation.2 | async-start | bytes 4194304 | tf_op jit(solution)/shard_map/all_to_all | solution.py:272
  122.8 28.3 %all-to-all-done.2 = bf16[128,12,512]{2,1,0:T(8,128)(2,1)S(1)} async-done(((bf16[128,12,512]{2,1,0:T(8,128)(2,1)}), bf16[128,12,512]{2,1,0:T(8,128)(2,1)S(1)}, u32[]{:S(2)}, u32[]{:S(2)}) %all-to-all-start.2) | async-done | bytes 1572896 | tf_op jit(solution)/shard_map/all_to_all | solution.py:272
  151.1 2.5 convert_select_fusion
  153.6 4.6 %reshape.193 = f32[1536,512]{1,0:T(8,128)} reshape(f32[128,12,512]{2,1,0:T(8,128)} %convert_select_fusion) | data formatting | bytes 6291456 | tf_op jit(solution)/shard_map/reshape | solution.py:275
  158.2 10.5 %scatter_custom_fusion.2 = f32[512,512]{1,0:T(8,128)S(1)} fusion(s32[1536]{0:T(1024)S(1)} %fusion.16, f32[1536,512]{1,0:T(8,128)} %reshape.193, f32[]{:T(128)} %constant.8.clone.1), kind=kCustom, calls=%fused_computation.32 | custom fusion | flops 786432 | bytes 1049088 | tf_op jit(solution)/shard_map/scatter-add | solution.py:276
  168.8 2.0 fusion.6
  170.8 1.5 fusion
  173.7 103.6 %all-reduce.6 = (f32[512,2048]{1,0:T(8,128)}, f32[512]{0:T(512)S(1)}) all-reduce(bf16[512,2048]{1,0:T(8,128)(2,1)} %get-tuple-element.11, f32[512]{0:T(512)S(1)} %bitcast.47), channel_id=1, replica_groups=mesh['user'=8,'item'=16] {'user','item'}, use_global_device_ids=true, to_apply=%region_8.9 | all-reduce | flops 1049088 | bytes 6295552 | tf_op jit(solution)/shard_map/psum | solution.py:270
  278.4 1.4 fusion.4
  279.9 41.3 %all-reduce.5.cloned.1.call-done = (f32[512,512]{0,1:T(8,128)}, f32[512,512]{1,0:T(8,128)}) async-done(((f32[512,512]{0,1:T(8,128)}, f32[512,512]{1,0:T(8,128)}), (f32[512,512]{0,1:T(8,128)}, f32[512,512]{1,0:T(8,128)})) %all-reduce.5.cloned.1.call-update) | async-done | bytes 2097168 | tf_op jit(solution)/shard_map/psum | solution.py:278
  321.2 2.6 copy.38
  (55 shorter events, 11.7 us)
Async XLA Ops:
  7.2 18.5 %copy-start = (bf16[512,512]{1,0:T(8,128)(2,1)S(1)}, bf16[512,512]{1,0:T(8,128)(2,1)}, u32[]{:S(2)}) copy-start(bf16[512,512]{1,0:T(8,128)(2,1)} %param.14) | copy-start | bytes 1572868
  7.2 2.3 copy-start.7
  7.2 18.0 %copy-start.1 = (bf16[512,512]{1,0:T(8,128)(2,1)S(1)}, bf16[512,512]{1,0:T(8,128)(2,1)}, u32[]{:S(2)}) copy-start(bf16[512,512]{1,0:T(8,128)(2,1)} %param.12) | copy-start | bytes 1572868
  7.2 18.0 %copy-start.2 = (bf16[512,512]{1,0:T(8,128)(2,1)S(1)}, bf16[512,512]{1,0:T(8,128)(2,1)}, u32[]{:S(2)}) copy-start(bf16[512,512]{1,0:T(8,128)(2,1)} %param.13) | copy-start | bytes 1572868
  13.7 21.0 %all-to-all-start = ((s32[128,1,12]{2,1,0:T(1,128)}), s32[128,1,12]{2,1,0:T(1,128)S(1)}, u32[]{:S(2)}, u32[]{:S(2)}) async-start(s32[128,1,12]{2,1,0:T(1,128)} %bitcast.4), calls=%async_computation | async-start | bytes 131072 | tf_op jit(solution)/shard_map/all_to_all | solution.py:252
  25.7 1.0 copy-start.4
  44.1 5.6 %copy-start.8 = (s32[1,768]{1,0:T(1,128)S(1)}, s32[1,768]{1,0:T(1,128)}, u32[]{:S(2)}) copy-start(s32[1,768]{1,0:T(1,128)} %param.23) | copy-start | bytes 9220
  44.1 6.6 %copy-start.9 = (s32[1,768]{1,0:T(1,128)S(1)}, s32[1,768]{1,0:T(1,128)}, u32[]{:S(2)}) copy-start(s32[1,768]{1,0:T(1,128)} %stamp_row_ref.1) | copy-start | bytes 9220
  44.1 35.2 %all-to-all-start.1 = ((bf16[128,12,512]{2,1,0:T(8,128)(2,1)}), bf16[128,12,512]{2,1,0:T(8,128)(2,1)}, u32[]{:S(2)}, u32[]{:S(2)}) async-start(bf16[128,12,512]{2,1,0:T(8,128)(2,1)} %broadcast_select_fusion), calls=%async_computation.1 | async-start | bytes 4194304 | tf_op jit(solution)/shard_map/all_to_all | solution.py:259
  116.8 34.4 %all-to-all-start.2 = ((bf16[128,12,512]{2,1,0:T(8,128)(2,1)}), bf16[128,12,512]{2,1,0:T(8,128)(2,1)S(1)}, u32[]{:S(2)}, u32[]{:S(2)}) async-start(bf16[128,12,512]{2,1,0:T(8,128)(2,1)} %reshape.155), calls=%async_computation.2 | async-start | bytes 4194304 | tf_op jit(solution)/shard_map/all_to_all | solution.py:272
  121.2 199.9 %all-reduce.5.cloned.1.call-start = ((), (), s32[]{:S(2)}) async-start(), calls=%async_computation.3 | async-start | bytes 4194304 | tf_op jit(solution)/shard_map/psum | solution.py:278
  168.7 2.0 copy-start.5
  172.2 1.5 copy-start.11
  173.7 103.7 %copy-start.10 = (f32[512]{0:T(512)S(1)}, f32[512]{0:T(512)}, u32[]{:S(2)}) copy-start(f32[512]{0:T(512)} %param.18) | copy-start | bytes 6148
  173.7 104.7 %copy-start.3 = (bf16[512,512]{1,0:T(8,128)(2,1)S(1)}, bf16[512,512]{1,0:T(8,128)(2,1)}, u32[]{:S(2)}) copy-start(bf16[512,512]{1,0:T(8,128)(2,1)} %param.13) | copy-start | bytes 1572868
  321.2 2.6 copy-start.6
Sparse Core Ops, SparseCore 0:
  173.8 147.3 all-reduce.4

commit v2 on v1

--- a/solution.py
+++ b/solution.py
@@ -17,6 +17,12 @@
 F32 = jnp.float32
 BF16 = jnp.bfloat16
 RB = 128
+OWNERS = 128
+SLOT = 16
+USED = 12
+PACK = 384
+ROWS = OWNERS * SLOT
+TILE = 256
 NEG = -1e30
 
 
@@ -32,14 +38,18 @@
     return 0.5 + 0.5 * jnp.tanh(0.5 * x)
 
 
+def column(row):
+    return jnp.broadcast_to(row.astype(F32), (128, row.shape[1])).T
+
+
 def keys_of(start):
     return min(HIST, start + RB)
 
 
 def hstu_kernel(
-    tok_ref, w1_ref, w2_ref, gain_ref, head_ref, tb_ref, stamp_row_ref, stamp_col_ref, label_ref,
+    tok_ref, w1_ref, w2_ref, gain_ref, head_ref, tb_ref, stamp_row_ref, label_ref,
     tgrad_ref, iterm_ref, uvec_ref, loss_ref,
-    normed, proj, dsl, idx, wts, dwt, att, dp, dkv,
+    normed, proj, dsl, idx, wts, dwt, att, dp,
 ):
     gain = gain_ref[...]
     head = head_ref[...]
@@ -63,10 +73,12 @@
     for k in range(BUCKETS):
         tab = tab + jnp.where(lane <= 31 - k, tb_ref[:, k : k + 1], 0.0)
     tab = jnp.where(lane == 33, NEG, tab)
+    stamp_col = column(stamp_row_ref[...]).astype(jnp.int32)
     for s in range(0, LOOK, RB):
         rows = pl.ds(s, RB)
         ke = keys_of(s)
-        gap = stamp_col_ref[rows, :] - stamp_row_ref[:, 0:ke]
+        now = jnp.concatenate([stamp_col[s : s + RB, :]] * (ke // 128), axis=1)
+        gap = now - stamp_row_ref[:, 0:ke]
         lz = lax.clz(gap + 1)
         if s < HIST:
             i_pos = s + lax.broadcasted_iota(jnp.int32, (RB, ke), 0)
@@ -113,6 +125,7 @@
     h_lo = (head - h_hi.astype(F32) - h_mid.astype(F32)).astype(BF16)
     parts = jnp.concatenate([h_hi, h_mid, h_lo, jnp.zeros((13, D), BF16)], axis=0)
     hw = jnp.sum(nt(parts, w2_ref[...]), axis=0, keepdims=True)
+    label_col = column(label_ref[...])
     loss = jnp.zeros((1, 1), F32)
     uvec = jnp.zeros((1, D), F32)
     dlogit = {}
@@ -126,7 +139,7 @@
         mixed = (n * g).astype(BF16).astype(F32)
         t = tok_ref[rows, :].astype(F32)
         logit = jnp.sum(t * head + mixed * hw, axis=1, keepdims=True)
-        lab = label_ref[rows, :].astype(F32)
+        lab = label_col[s : s + RB, 0:1]
         soft = jnp.maximum(logit, 0.0) + jnp.log1p(jnp.exp(-jnp.abs(logit)))
         loss = loss + jnp.sum(soft - lab * logit, axis=0, keepdims=True)
         dl = (jax.nn.sigmoid(logit) - lab) * (1.0 / LOOK)
@@ -186,7 +199,7 @@
     nrt = normed[...].astype(F32).T.astype(BF16)
     for c in range(0, 4 * D, 256):
         cols = pl.ds(c, 256)
-        iterm_ref[:, cols] = nn(nrt, dp[:, cols]).astype(BF16)
+        iterm_ref[c // D, :, pl.ds(c % D, 256)] = nn(nrt, dp[:, cols]).astype(BF16)
 
 
 def hstu(tok, w1, w2, gain, head, tb, stamps, labels):
@@ -195,11 +208,11 @@
         hstu_kernel,
         out_shape=(
             jax.ShapeDtypeStruct((LOOK, D), BF16),
-            jax.ShapeDtypeStruct((D, 4 * D), BF16),
+            jax.ShapeDtypeStruct((4, D, D), BF16),
             jax.ShapeDtypeStruct((1, D), F32),
             jax.ShapeDtypeStruct((1, 128), F32),
         ),
-        in_specs=[vm] * 9,
+        in_specs=[vm] * 8,
         out_specs=(vm,) * 4,
         scratch_shapes=[
             pltpu.VMEM((LOOK, D), BF16),
@@ -210,75 +223,481 @@
             pltpu.VMEM((HEADS, LOOK, HIST), BF16),
             pltpu.VMEM((LOOK, D), F32),
             pltpu.VMEM((LOOK, 4 * D), BF16),
-            pltpu.VMEM((8, 128), F32),
         ],
         compiler_params=pltpu.CompilerParams(vmem_limit_bytes=56 * 2**20),
         cost_estimate=pl.CostEstimate(flops=8 * 10**9, bytes_accessed=8 * 2**20, transcendentals=4 * 10**6),
         name="hstu",
     )(
         tok, w1, w2, gain.reshape(1, D), head.reshape(1, D), tb,
-        stamps.reshape(1, LOOK), stamps.reshape(LOOK, 1), labels.reshape(LOOK, 1),
+        stamps.reshape(1, LOOK), labels.reshape(1, LOOK),
     )
 
 
-def tower_block(item_rows, first, second):
-    hidden_items = jax.nn.silu(
-        jnp.dot(item_rows.astype(jnp.bfloat16), first, preferred_element_type=jnp.float32)
-    ).astype(jnp.bfloat16)
-    return item_rows + jnp.dot(hidden_items, second, preferred_element_type=jnp.float32)
+def place():
+    return lax.axis_index("user"), lax.axis_index("item")
+
+
+def device(index):
+    return (index // 16, index % 16)
+
+
+def greet(me):
+    barrier = pltpu.get_barrier_semaphore()
+
+    @pl.loop(1, OWNERS)
+    def _(k):
+        pl.semaphore_signal(
+            barrier, inc=1, device_id=device((me + k) % OWNERS), device_id_type=pl.DeviceIdType.MESH
+        )
+
+
+def meet():
+    pl.semaphore_wait(pltpu.get_barrier_semaphore(), OWNERS - 1)
+
+
+def row_in_slot(n):
+    return lax.broadcasted_iota(jnp.int32, (n, 128), 0) % SLOT
+
+
+def pack(y):
+    r = row_in_slot(y.shape[0])
+    last = y[:, PACK:D]
+    out = [
+        jnp.where(r >= USED, pltpu.roll(last, USED - 4 * b, 0), y[:, 128 * b : 128 * (b + 1)])
+        for b in range(3)
+    ]
+    return jnp.concatenate(out, axis=1).astype(BF16)
+
+
+def unpack_last(y):
+    n = y.shape[0]
+    r = row_in_slot(n)
+    p = [pltpu.roll(y[:, 128 * b : 128 * (b + 1)].astype(F32), n - USED + 4 * b, 0) for b in range(3)]
+    return jnp.where(r < 4, p[0], jnp.where(r < 8, p[1], p[2])).astype(BF16)
+
+
+def chunk(ref, k):
+    return ref.at[pl.ds(pl.multiple_of(k * SLOT, SLOT), SLOT), :]
+
+
+def send_chunk(send, recv, k, target, send_sem, recv_sem):
+    pltpu.make_async_remote_copy(
+        src_ref=chunk(send, k),
+        dst_ref=chunk(recv, k),
+        send_sem=send_sem,
+        recv_sem=recv_sem,
+        device_id=device(target),
+        device_id_type=pl.DeviceIdType.MESH,
+    ).start()
+
+
+def wait_bytes(ref, sem):
+    pltpu.make_async_copy(ref, ref, sem).wait()
+
+
+def silu_parts(p):
+    sg = sigmoid(p)
+    y = p * sg
+    return y, sg + y * (1.0 - sg)
+
+
+def front_kernel(
+    owner_ref, row_ref, table_ref, first_ref, second_ref,
+    tok_ref, slot_ref, idrow_ref,
+    ids_send, ids_recv, embed, idq, send, recv, last, sems,
+):
+    user, item = place()
+    me = user * 16 + item
+    greet(me)
+    j_row = (owner_ref[...] - me + OWNERS) % OWNERS
+    named = lax.broadcasted_iota(jnp.int32, (OWNERS, LOOK), 0) == j_row
+    named_b = named.astype(F32).astype(BF16)
+    before = lax.broadcasted_iota(jnp.int32, (LOOK, LOOK), 0) < lax.broadcasted_iota(
+        jnp.int32, (LOOK, LOOK), 1
+    )
+    earlier = nn(named_b, before.astype(F32).astype(BF16))
+    rank = jnp.sum(jnp.where(named, earlier, 0.0), axis=0, keepdims=True)
+    slot_ref[...] = j_row * SLOT + rank.astype(jnp.int32)
+    lanes = lax.broadcasted_iota(jnp.int32, (LOOK, 128), 1).astype(F32)
+    listed = jnp.where(column(rank) == lanes, column(row_ref[...]) - 256.0, 0.0)
+    ids_send[:, 0, :] = nn(named_b, listed.astype(BF16))
+    ids_recv[0] = ids_send[0]
+    meet()
+
+    def ids_copy(k):
+        return pltpu.make_async_remote_copy(
+            src_ref=ids_send.at[k],
+            dst_ref=ids_recv.at[k],
+            send_sem=sems.at[0],
+            recv_sem=sems.at[1],
+            device_id=device((me + k) % OWNERS),
+            device_id_type=pl.DeviceIdType.MESH,
+        )
+
+    @pl.loop(1, OWNERS)
+    def _(k):
+        ids_copy(k).start()
+
+    for s in range(0, D, 256):
+        rows = pl.ds(s, 256)
+        hidden, _ = silu_parts(nn(table_ref[rows, :], first_ref[...]))
+        embed[rows, :] = (
+            table_ref[rows, :].astype(F32) + nn(hidden.astype(BF16), second_ref[...])
+        ).astype(BF16)
+    others = pl.ds(1, OWNERS - 1)
+    wait_bytes(ids_recv.at[others], sems.at[1])
+    wait_bytes(ids_send.at[others], sems.at[0])
+    ids = ids_recv[:, 0, :].astype(BF16)
+
+    @pl.loop(0, ROWS // TILE)
+    def _(t):
+        base = t * TILE
+        rows = pl.ds(pl.multiple_of(base, TILE), TILE)
+        at = base + lax.broadcasted_iota(jnp.int32, (TILE, 128), 0)
+        lane = lax.broadcasted_iota(jnp.int32, (TILE, 128), 1)
+        spread = nn((at // SLOT == lane).astype(F32).astype(BF16), ids)
+        r = at % SLOT
+        mine = jnp.sum(jnp.where(r == lane, spread + 256.0, 0.0), axis=1, keepdims=True)
+        mine = jnp.where(r < USED, mine, -1.0)
+        idq[rows, :] = mine
+        cols = lax.broadcasted_iota(jnp.int32, (TILE, 128), 1).astype(F32)
+        pick = jnp.concatenate(
+            [(mine == cols + 128.0 * b).astype(F32).astype(BF16) for b in range(4)], axis=1
+        )
+        send[rows, :] = pack(nn(pick, embed[...]))
+
+        @pl.loop(0, TILE // SLOT)
+        def _(i):
+            k = t * (TILE // SLOT) + i
+
+            @pl.when(k > 0)
+            def _():
+                send_chunk(send, recv, k, (me - k + OWNERS) % OWNERS, sems.at[2], sems.at[3])
+
+    recv[0:SLOT, :] = send[0:SLOT, :]
+    idrow_ref[...] = idq[...].T[0:8, :]
+    slot_col = column(slot_ref[...])
+    later = pl.ds(SLOT, ROWS - SLOT)
+    wait_bytes(recv.at[later], sems.at[3])
+    for s in range(0, ROWS, TILE):
+        rows = pl.ds(s, TILE)
+        last[rows, :] = unpack_last(recv[rows, :])
+    for s in range(0, LOOK, RB):
+        rows = pl.ds(s, RB)
+        mark = slot_col[s : s + RB, :]
+        cols = lax.broadcasted_iota(jnp.int32, (RB, 128), 1).astype(F32)
+        pick = jnp.concatenate(
+            [(mark == cols + float(b)).astype(F32).astype(BF16) for b in range(0, ROWS, 128)],
+            axis=1,
+        )
+        tok_ref[rows, 0:PACK] = nn(pick, recv[...]).astype(BF16)
+        tok_ref[rows, PACK:D] = nn(pick, last[...]).astype(BF16)
+    wait_bytes(send.at[later], sems.at[2])
+
+
+VM = pl.BlockSpec(memory_space=pltpu.VMEM)
+
+
+def front(owner, row, table, first, second):
+    return pl.pallas_call(
+        front_kernel,
+        out_shape=(
+            jax.ShapeDtypeStruct((LOOK, D), BF16),
+            jax.ShapeDtypeStruct((1, LOOK), jnp.int32),
+            jax.ShapeDtypeStruct((8, ROWS), F32),
+        ),
+        in_specs=[VM] * 5,
+        out_specs=(VM,) * 3,
+        scratch_shapes=[
+            pltpu.VMEM((OWNERS, 1, 128), F32),
+            pltpu.VMEM((OWNERS, 1, 128), F32),
+            pltpu.VMEM((D, D), BF16),
+            pltpu.VMEM((ROWS, 128), F32),
+            pltpu.VMEM((ROWS, PACK), BF16),
+            pltpu.VMEM((ROWS, PACK), BF16),
+            pltpu.VMEM((ROWS, 128), BF16),
+            pltpu.SemaphoreType.DMA((4,)),
+        ],
+        compiler_params=pltpu.CompilerParams(
+            vmem_limit_bytes=48 * 2**20, collective_id=0, has_side_effects=True
+        ),
+        cost_estimate=pl.CostEstimate(
+            flops=4 * 10**9, bytes_accessed=8 * 2**20, transcendentals=10**6
+        ),
+        name="front",
+    )(owner, row, table, first, second)
+
+
+BLOCKS = 6
+EARLY = (0, 1, 2, 3)
+LATE = (4, 5)
+ORDER = ("xyz", "yzx", "zxy", "xyz", "yzx", "zxy")
+H1 = D // 8
+H2 = H1 // 4
+
+
+def back_kernel(
+    tgrad_ref, slot_ref, idrow_ref, iterm_ref, uvec_ref, table_ref, first_ref, second_ref,
+    tablegrad_ref, sums_ref, usum_ref,
+    send, recv, last, terms, core_in, half, in1, part1, in2, part2, in3, u_held, u_in,
+    hidden_t, table_t, slope,
+    sems, send_sems, recv_sems, u_sems,
+):
+    user, item = place()
+    me = user * 16 + item
+    greet(me)
+    z, core = user // 2, user % 2
+    x, y = item // 4, item % 4
+    own = {"x": x, "y": y, "z": z}
+
+    def peer(axis, d):
+        if axis == "c":
+            return (z * 2 + 1 - core, item)
+        to = (own[axis] + d) % 4
+        if axis == "x":
+            return (user, to * 4 + y)
+        if axis == "y":
+            return (user, x * 4 + to)
+        return (to * 2 + core, item)
+
+    def copy(src, dst, to, send_sem, recv_sem):
+        return pltpu.make_async_remote_copy(
+            src_ref=src, dst_ref=dst, send_sem=send_sem, recv_sem=recv_sem,
+            device_id=to, device_id_type=pl.DeviceIdType.MESH,
+        )
+
+    def at(n, size):
+        return pl.ds(pl.multiple_of(n * size, size), size)
+
+    def term(b):
+        return iterm_ref.at[b] if b in EARLY else terms.at[b - 4]
+
+    def copies(b, stage):
+        if stage in (0, 7):
+            if stage == 0:
+                src, dst = term(b).at[at(1 - core, 256), :], core_in.at[b]
+            else:
+                src = dst = sums_ref.at[b, at(core, 256), :]
+            return [copy(src, dst, peer("c", 1), send_sems.at[b, stage, 0], recv_sems.at[b, stage, 0])]
+        axes = ORDER[b]
+        a0, a1, a2 = (own[a] for a in axes)
+        step = stage - 1 if stage < 4 else 6 - stage
+        out = []
+        for d in (1, 2, 3):
+            to = (own[axes[step]] + d) % 4
+            if stage == 1:
+                src, dst = half.at[b, at(to, 64), :], in1.at[b, d - 1]
+            elif stage == 2:
+                src, dst = part1.at[b, :, at(to, 128)], in2.at[b, d - 1]
+            elif stage == 3:
+                src, dst = part2.at[b, at(to, 16), :], in3.at[b, d - 1]
+            elif stage == 4:
+                src = dst = sums_ref.at[b, pl.ds(pl.multiple_of(core * 256 + a0 * 64 + a2 * 16, 16), 16), at(a1, 128)]
+            elif stage == 5:
+                src = dst = sums_ref.at[b, pl.ds(pl.multiple_of(core * 256 + a0 * 64, 64), 64), at(a1, 128)]
+            else:
+                src = dst = sums_ref.at[b, pl.ds(pl.multiple_of(core * 256 + a0 * 64, 64), 64), :]
+            out.append(
+                copy(src, dst, peer(axes[step], d), send_sems.at[b, stage, d - 1], recv_sems.at[b, stage, d - 1])
+            )
+        return out
+
+    def start(b, stage):
+        for c in copies(b, stage):
+            c.start()
+
+    def finish(b, stage):
+        for c in copies(b, stage):
+            c.wait_recv()
+        a0, a1, a2 = (own[a] for a in ORDER[b])
+        if stage == 0:
+            half[b] = (term(b)[at(core, 256), :].astype(F32) + core_in[b].astype(F32)).astype(BF16)
+        elif stage == 1:
+            part1[b] = add4(half[b, at(a0, 64), :], in1, b)
+        elif stage == 2:
+            part2[b] = add4(part1[b, :, at(a1, 128)], in2, b)
+        elif stage == 3:
+            rows = pl.ds(pl.multiple_of(core * 256 + a0 * 64 + a2 * 16, 16), 16)
+            sums_ref[b, rows, at(a1, 128)] = add4(part2[b, at(a2, 16), :], in3, b)
+
+    def add4(mine, arrived, b):
+        total = mine.astype(F32)
+        for d in range(3):
+            total = total + arrived[b, d].astype(F32)
+        return total.astype(BF16)
+
+    def u_copies(stage):
+        axis = "cxyz"[stage]
+        return [
+            copy(u_held.at[stage], u_in.at[stage, d - 1], peer(axis, d), u_sems.at[0, stage, d - 1], u_sems.at[1, stage, d - 1])
+            for d in ((1,) if stage == 0 else (1, 2, 3))
+        ]
+
+    def u_start(stage):
+        for c in u_copies(stage):
+            c.start()
+
+    def u_finish(stage):
+        total = u_held[stage]
+        for d, c in enumerate(u_copies(stage)):
+            c.wait_recv()
+            total = total + u_in[stage, d]
+        if stage < 3:
+            u_held[stage + 1] = total
+        else:
+            usum_ref[...] = total
+
+    slots = slot_ref[...]
+    tgrad = tgrad_ref[...]
+
+    @pl.loop(0, ROWS // TILE)
+    def _(t):
+        base = t * TILE
+        rows = pl.ds(pl.multiple_of(base, TILE), TILE)
+        pick = base + lax.broadcasted_iota(jnp.int32, (TILE, LOOK), 0) == slots
+        send[rows, :] = pack(nn(pick.astype(F32).astype(BF16), tgrad))
+
+    u_held[0] = uvec_ref[...]
+    recv[0:SLOT, :] = send[0:SLOT, :]
+    meet()
+    for b in EARLY:
+        start(b, 0)
+    u_start(0)
+
+    @pl.loop(1, OWNERS)
+    def _(k):
+        send_chunk(send, recv, k, (me + k) % OWNERS, sems.at[0], sems.at[1])
+
+    for s in range(0, D, 256):
+        rows = pl.ds(s, 256)
+        tab = table_ref[rows, :]
+        hidden, dh = silu_parts(nn(tab, first_ref[...]))
+        slope[rows, :] = dh
+        hidden_t[:, rows] = hidden.T.astype(BF16)
+        table_t[:, rows] = tab.astype(F32).T.astype(BF16)
+    for b in EARLY:
+        finish(b, 0)
+        start(b, 1)
+    u_finish(0)
+    u_start(1)
+    later = pl.ds(SLOT, ROWS - SLOT)
+    wait_bytes(recv.at[later], sems.at[1])
+    for s in range(0, ROWS, TILE):
+        rows = pl.ds(s, TILE)
+        last[rows, :] = unpack_last(recv[rows, :])
+    for s in range(0, D, 128):
+        rows = pl.ds(s, 128)
+        sub = (s + lax.broadcasted_iota(jnp.int32, (128, 128), 0)).astype(F32)
+        pick = jnp.concatenate(
+            [
+                (sub == idrow_ref[0:1, q : q + 128]).astype(F32).astype(BF16)
+                for q in range(0, ROWS, 128)
+            ],
+            axis=1,
+        )
+        tablegrad_ref[rows, 0:PACK] = nn(pick, recv[...])
+        tablegrad_ref[rows, PACK:D] = nn(pick, last[...])
+    de = tablegrad_ref[...].astype(BF16)
+    terms[1] = nn(hidden_t[...], de).astype(BF16)
+    start(5, 0)
+    dpre = (nt(de, second_ref[...]) * slope[...]).astype(BF16)
+    terms[0] = nn(table_t[...], dpre).astype(BF16)
+    start(4, 0)
+    for b in EARLY:
+        finish(b, 1)
+        start(b, 2)
+    u_finish(1)
+    u_start(2)
+    tablegrad_ref[...] += nt(dpre, first_ref[...])
+    for b in LATE:
+        finish(b, 0)
+        start(b, 1)
+    for stage in range(2, 7):
+        for b in EARLY:
+            finish(b, stage)
+            start(b, stage + 1)
+        if stage < 4:
+            u_finish(stage)
+        if stage < 3:
+            u_start(stage + 1)
+        for b in LATE:
+            finish(b, stage - 1)
+            start(b, stage)
+    for b in LATE:
+        finish(b, 6)
+        start(b, 7)
+    for b in EARLY + LATE:
+        finish(b, 7)
+    wait_bytes(send.at[later], sems.at[0])
+    for stage in range(4):
+        for c in u_copies(stage):
+            c.wait_send()
+    for b in EARLY + LATE:
+        for stage in range(8):
+            for c in copies(b, stage):
+                c.wait_send()
+
+
+def back(tgrad, slots, idrow, iterm, uvec, table, first, second):
+    dma = pltpu.SemaphoreType.DMA
+    return pl.pallas_call(
+        back_kernel,
+        out_shape=(
+            jax.ShapeDtypeStruct((D, D), F32),
+            jax.ShapeDtypeStruct((BLOCKS, D, D), BF16),
+            jax.ShapeDtypeStruct((1, D), F32),
+        ),
+        in_specs=[VM] * 8,
+        out_specs=(VM,) * 3,
+        scratch_shapes=[
+            pltpu.VMEM((ROWS, PACK), BF16),
+            pltpu.VMEM((ROWS, PACK), BF16),
+            pltpu.VMEM((ROWS, 128), BF16),
+            pltpu.VMEM((2, D, D), BF16),
+            pltpu.VMEM((BLOCKS, 256, D), BF16),
+            pltpu.VMEM((BLOCKS, 256, D), BF16),
+            pltpu.VMEM((BLOCKS, 3, 64, D), BF16),
+            pltpu.VMEM((BLOCKS, 64, D), BF16),
+            pltpu.VMEM((BLOCKS, 3, 64, 128), BF16),
+            pltpu.VMEM((BLOCKS, 64, 128), BF16),
+            pltpu.VMEM((BLOCKS, 3, 16, 128), BF16),
+            pltpu.VMEM((4, 1, D), F32),
+            pltpu.VMEM((4, 3, 1, D), F32),
+            pltpu.VMEM((D, D), BF16),
+            pltpu.VMEM((D, D), BF16),
+            pltpu.VMEM((D, D), F32),
+            dma((2,)),
+            dma((BLOCKS, 8, 3)),
+            dma((BLOCKS, 8, 3)),
+            dma((2, 4, 3)),
+        ],
+        compiler_params=pltpu.CompilerParams(
+            vmem_limit_bytes=48 * 2**20, collective_id=1, has_side_effects=True
+        ),
+        cost_estimate=pl.CostEstimate(
+            flops=4 * 10**9, bytes_accessed=8 * 2**20, transcendentals=10**6
+        ),
+        name="back",
+    )(tgrad, slots, idrow, iterm, uvec, table, first, second)
 
 
 def body(
     table, tower_first, tower_second, w_input, w_output, norm_gain, head_vec, time_bias,
     look_owner, look_row, event_time, labels,
 ):
-    n_user = lax.axis_size("user")
-    n_item = lax.axis_size("item")
-    owners = n_user * n_item
-    lookups = look_row.shape[1]
-    features = table.shape[1]
-    capacity = 12
-    owner_ids = look_owner[0, :, 0]
-    targets = jnp.arange(owners, dtype=jnp.int32)
-    onehot = (owner_ids[:, None] == targets[None, :]).astype(jnp.int32)
-    position = jnp.sum(onehot * (jnp.cumsum(onehot, axis=0) - 1), axis=1)
-    slot_index = owner_ids * capacity + position
-    send_ids = (
-        jnp.full((owners * capacity,), -1, jnp.int32)
-        .at[slot_index]
-        .set(look_row[0])
-        .reshape(owners, capacity)
+    tok, slots, idrow = front(
+        look_owner.reshape(1, LOOK), look_row, table, tower_first, tower_second
     )
-    recv_ids = lax.all_to_all(send_ids, ("user", "item"), split_axis=0, concat_axis=0, tiled=True)
-    item_rows = table.astype(jnp.float32)
-    embed_f, tower_back = jax.vjp(tower_block, item_rows, tower_first, tower_second)
-    embedding = embed_f.astype(jnp.bfloat16)
-    is_live = recv_ids >= 0
-    safe_rows = jnp.where(is_live, recv_ids, 0)
-    replies = jnp.where(is_live[:, :, None], embedding[safe_rows], jnp.zeros((), jnp.bfloat16))
-    back_rows = lax.all_to_all(replies, ("user", "item"), split_axis=0, concat_axis=0, tiled=True)
-    tok = back_rows.reshape(owners * capacity, features)[slot_index]
-    token_grad, input_term, uvec, loss = hstu(
+    tgrad, iterm, uvec, loss = hstu(
         tok, w_input, w_output, norm_gain, head_vec, time_bias, event_time, labels
     )
-    send_grad = (
-        jnp.zeros((owners * capacity, features), BF16)
-        .at[slot_index]
-        .set(token_grad)
-        .reshape(owners, capacity, features)
+    table_grad, sums, usum = back(
+        tgrad, slots, idrow, iterm, uvec, table, tower_first, tower_second
     )
-    input_grad, uvec = lax.psum((input_term.astype(F32), uvec[0]), ("user", "item"))
-    output_grad = uvec[:, None] * head_vec[None, :]
-    recv_grad = lax.all_to_all(
-        send_grad, ("user", "item"), split_axis=0, concat_axis=0, tiled=True
-    ).astype(F32)
-    live_grad = jnp.where(is_live[:, :, None], recv_grad, 0.0).reshape(owners * capacity, features)
-    embed_grad = jnp.zeros_like(item_rows).at[safe_rows.reshape(-1)].add(live_grad)
-    table_grad, first_term, second_term = tower_back(embed_grad)
-    first_grad, second_grad = lax.psum(
-        (first_term.astype(F32), second_term.astype(F32)), ("user", "item")
-    )
-    return (table_grad, first_grad, second_grad, input_grad, output_grad, loss[0, :1])
+    sums = sums.astype(F32)
+    input_grad = jnp.concatenate([sums[b] for b in range(4)], axis=1)
+    output_grad = usum[0][:, None] * head_vec[None, :]
+    return (table_grad, sums[4], sums[5], input_grad, output_grad, loss[0, :1])
 
 
 def solution(mesh):

time: 337 us -> 157 us (0.47); the launches traced: 332 us -> 156 us
  Pallas kernels: 23.2 us -> 138 us
  waiting for transfers between devices: 105 us -> 0 us
  blocking collectives: 104 us -> 0 us
  local copies, waits for them, and re-layouts: 36.5 us -> 11.8 us
  starting transfers between devices: 21.6 us -> 0 us
  between operations: 14.6 us -> 0.7 us
  other arithmetic: 19.8 us -> 6.14 us
  matrix products: 7.21 us -> 0 us
    pallas_call x0 -> x2, Pallas kernels: none -> 115 us  [the longest x1 67.7 us: back(): pl.pallas_call(back_kernel, out_shape=(jax.ShapeDtypeStruct((D, D), F32),...]
    psum x1 -> x0, blocking collectives: 104 us -> none  [body(): lax.psum((input_term.astype(F32), uvec[0]), ('user', 'item'))]
    all_to_all x3 -> x0, waiting for transfers between devices: 64 us -> none  [the longest x1 28.3 us: body(): lax.all_to_all(send_grad, ('user', 'item'), split_axis=0, concat_axis=0,...]
    psum x1 -> x0, waiting for transfers between devices: 41.3 us -> none  [body(): lax.psum((first_term.astype(F32), second_term.astype(F32)), ('user', 'ite...]
    all_to_all x3 -> x0, starting transfers between devices: 21.6 us -> none  [the longest x1 11.5 us: body(): lax.all_to_all(send_ids, ('user', 'item'), split_axis=0, concat_axis=0, t...]
    scatter-add x1 -> x0, other arithmetic: 10.5 us -> none  [body(): jnp.zeros_like(item_rows).at[safe_rows.reshape(-1)].add(live_grad)]
    reshape x5 -> x0, local copies, waits for them, and re-layouts: 10.5 us -> none  [the longest x1 4.61 us: body(): jnp.where(is_live[:, :, None], recv_grad, 0.0)]
    gather x3 -> x0, local copies, waits for them, and re-layouts: 10.1 us -> none  [the longest x2 6.32 us: body(): embedding[safe_rows]]
  transfers between devices with their start and end apart: 4 -> 0, of which waited for: 4 -> 0; matrix products, arithmetic and copies ran while one was open for 2% -> 0% of each run, Pallas kernels for 0% -> 0%
where the time goes in v2:
time: 157 us; the launch traced here: 156 us
  Pallas kernels  138 us (88%)
  local copies, waits for them, and re-layouts  11.8 us (8%)
  other arithmetic  6.14 us (4%)
    pallas_call x1, Pallas kernels, back(): pl.pallas_call(back_kernel, out_shape=(jax.ShapeDtypeStruct((D, D), F32),...  67.7 us
    pallas_call x1, Pallas kernels, front(): pl.pallas_call(front_kernel, out_shape=(jax.ShapeDtypeStruct((LOOK, D), B...  47 us
    pallas_call x1, Pallas kernels, hstu(): pl.pallas_call(hstu_kernel, out_shape=(jax.ShapeDtypeStruct((LOOK, D), BF...  23.1 us
    unnamed x27, local copies, waits for them, and re-layouts  9.74 us

profile of v2, /device:TPU:1, one launch (start us, length us, event | category | flops | bytes accessed | tf_op | source)
XLA Modules:
  0.0 156.5 jit_solution(5631515642926070640)
XLA Ops:
  0.6 0.0 copy-start
  0.6 1.0 copy-done
  1.7 1.0 copy-done.2
  2.7 1.0 copy-done.4
  3.8 0.7 copy-done.6
  4.4 0.7 copy-done.7
  5.1 47.0 %front.1 = (bf16[768,512]{1,0:T(8,128)(2,1)S(1)}, s32[1,768]{1,0:T(1,128)S(1)}, f32[8,2048]{1,0:T(8,128)S(1)}) custom-call(s32[1,768]{1,0:T(1,128)S(1)} %bitcast.19, s32[1,768]{1,0:T(1,128)S(1)} %copy-done.7, bf16[512,512]{1,0:T(8,128)(2,1)S(1)} %copy-done, bf16[512,512]{1,0:T(8,128)(2,1)S(1)} %copy-done.2, bf16[512,512]{1,0:T(8,128)(2,1)S(1)} %copy-done.4), custom_call_target="tpu_custom_call" | custom-call | flops 4000000000 | bytes 8388608 | tf_op jit(solution)/shard_map/front/pallas_call | solution.py:402
  52.2 0.0 copy-start.10
  52.2 0.9 copy-done.10
  53.1 23.1 %hstu.1 = (bf16[768,512]{1,0:T(8,128)(2,1)}, bf16[4,512,512]{2,1,0:T(8,128)(2,1)}, f32[1,512]{1,0:T(1,128)}, f32[1,128]{1,0:T(1,128)}) custom-call(bf16[768,512]{1,0:T(8,128)(2,1)} %copy-done.10, bf16[512,2048]{1,0:T(8,128)(2,1)} %w1_ref.1, bf16[512,512]{1,0:T(8,128)(2,1)} %w2_ref.1, f32[1,512]{1,0:T(1,128)} %bitcast.21, f32[1,512]{1,0:T(1,128)} %bitcast.20, ...), custom_call_target="tpu_custom_call" | custom-call | flops 8000000000 | bytes 8388608 | tf_op jit(solution)/shard_map/hstu/pallas_call | solution.py:207
  76.1 0.0 copy-done.1
  76.1 0.0 copy-done.3
  76.1 0.0 copy-done.5
  76.2 0.0 copy-start.8
  76.2 1.6 %copy-done.8 = bf16[4,512,512]{2,1,0:T(8,128)(2,1)S(1)} copy-done((bf16[4,512,512]{2,1,0:T(8,128)(2,1)S(1)}, bf16[4,512,512]{2,1,0:T(8,128)(2,1)}, u32[]{:S(2)}) %copy-start.8) | copy-done | bytes 2097176
  77.8 1.1 copy-done.9
  78.9 0.7 copy-done.11
  79.6 67.7 %back.1 = (f32[512,512]{1,0:T(8,128)S(1)}, bf16[6,512,512]{2,1,0:T(8,128)(2,1)}, f32[1,512]{1,0:T(1,128)S(1)}) custom-call(bf16[768,512]{1,0:T(8,128)(2,1)S(1)} %copy-done.9, s32[1,768]{1,0:T(1,128)S(1)} %get-tuple-element.18.slot_ref, f32[8,2048]{1,0:T(8,128)S(1)} %get-tuple-element.19.idrow_ref, bf16[4,512,512]{2,1,0:T(8,128)(2,1)S(1)} %copy-done.8, ...), custom_call_target="tpu_custom_call" | custom-call | flops 4000000000 | bytes 8388608 | tf_op jit(solution)/shard_map/back/pallas_call | solution.py:643
  147.3 2.8 %convert_element_type.3 = f32[6,512,512]{2,1,0:T(8,128)S(1)} convert(bf16[6,512,512]{2,1,0:T(8,128)(2,1)} %get-tuple-element.23) | non-fusion elementwise | flops 1572864 | bytes 9437184 | tf_op jit(solution)/shard_map/convert_element_type | solution.py:697
  150.1 2.0 %slice_bitcast_fusion.3 = (f32[512,512]{1,0:T(8,128)S(1)}, f32[512,512]{1,0:T(8,128)S(1)}, f32[512,512]{1,0:T(8,128)S(1)}, f32[512,512]{1,0:T(8,128)S(1)}, f32[512,512]{1,0:T(8,128)}, /*index=5*/f32[512,512]{1,0:T(8,128)}) fusion(f32[6,512,512]{2,1,0:T(8,128)S(1)} %convert_element_type.3), kind=kLoop, calls=%fused_computation.4 | loop fusion | bytes 12582912 | tf_op jit(solution)/shard_map/squeeze | solution.py:698
  152.1 2.3 %pad_maximum_fusion = f32[512,2048]{1,0:T(8,128)} fusion(f32[512,512]{1,0:T(8,128)S(1)} %get-tuple-element.27, f32[512,512]{1,0:T(8,128)S(1)} %get-tuple-element.28, f32[512,512]{1,0:T(8,128)S(1)} %get-tuple-element.29, f32[512,512]{1,0:T(8,128)S(1)} %get-tuple-element.26), kind=kLoop, calls=%fused_computation | loop fusion | flops 3145728 | bytes 8388608 | tf_op jit(solution)/shard_map/concatenate | solution.py:698
  154.4 0.0 copy-done.12
  154.4 1.1 broadcast_multiply_fusion
  155.5 1.0 copy.19
  (10 shorter events, 0.0 us)
Async XLA Ops:
  0.6 1.0 copy-start
  1.7 1.0 copy-start.2
  2.7 1.0 copy-start.4
  3.8 0.7 copy-start.6
  4.4 0.7 copy-start.7
  52.2 0.9 copy-start.10
  53.0 23.1 %copy-start.1 = (bf16[512,512]{1,0:T(8,128)(2,1)S(1)}, bf16[512,512]{1,0:T(8,128)(2,1)}, u32[]{:S(2)}) copy-start(bf16[512,512]{1,0:T(8,128)(2,1)} %table_ref.3) | copy-start | bytes 1572868
  53.1 23.1 %copy-start.3 = (bf16[512,512]{1,0:T(8,128)(2,1)S(1)}, bf16[512,512]{1,0:T(8,128)(2,1)}, u32[]{:S(2)}) copy-start(bf16[512,512]{1,0:T(8,128)(2,1)} %first_ref.3) | copy-start | bytes 1572868
  53.1 23.1 %copy-start.5 = (bf16[512,512]{1,0:T(8,128)(2,1)S(1)}, bf16[512,512]{1,0:T(8,128)(2,1)}, u32[]{:S(2)}) copy-start(bf16[512,512]{1,0:T(8,128)(2,1)} %second_ref.3) | copy-start | bytes 1572868
  76.2 1.6 %copy-start.8 = (bf16[4,512,512]{2,1,0:T(8,128)(2,1)S(1)}, bf16[4,512,512]{2,1,0:T(8,128)(2,1)}, u32[]{:S(2)}) copy-start(bf16[4,512,512]{2,1,0:T(8,128)(2,1)} %get-tuple-element.20.iterm_ref) | copy-start | bytes 6291460
  77.8 1.1 copy-start.9
  78.9 0.7 copy-start.11
  152.1 2.3 %copy-start.12 = (f32[512]{0:T(512)S(1)}, f32[512]{0:T(512)}, u32[]{:S(2)}) copy-start(f32[512]{0:T(512)} %param.18) | copy-start | bytes 6148

commit v3 on v1

--- a/solution.py
+++ b/solution.py
@@ -17,6 +17,14 @@
 F32 = jnp.float32
 BF16 = jnp.bfloat16
 RB = 128
+OWNERS = 128
+SLOT = 16
+USED = 12
+PACK = 384
+ROWS = OWNERS * SLOT
+TILE = 512
+STEP = 37
+UNSTEP = 45
 NEG = -1e30
 
 
@@ -32,18 +40,202 @@
     return 0.5 + 0.5 * jnp.tanh(0.5 * x)
 
 
+def column(row):
+    return jnp.broadcast_to(row.astype(F32), (128, row.shape[1])).T
+
+
 def keys_of(start):
     return min(HIST, start + RB)
 
 
-def hstu_kernel(
-    tok_ref, w1_ref, w2_ref, gain_ref, head_ref, tb_ref, stamp_row_ref, stamp_col_ref, label_ref,
-    tgrad_ref, iterm_ref, uvec_ref, loss_ref,
-    normed, proj, dsl, idx, wts, dwt, att, dp, dkv,
+def place():
+    return lax.axis_index("user"), lax.axis_index("item")
+
+
+def device(index):
+    return (index // 16, index % 16)
+
+
+def greet(me):
+    barrier = pltpu.get_barrier_semaphore()
+
+    @pl.loop(1, OWNERS)
+    def _(k):
+        pl.semaphore_signal(
+            barrier, inc=1, device_id=device((me + k) % OWNERS), device_id_type=pl.DeviceIdType.MESH
+        )
+
+
+def meet():
+    pl.semaphore_wait(pltpu.get_barrier_semaphore(), OWNERS - 1)
+
+
+def row_in_slot(n):
+    return lax.broadcasted_iota(jnp.int32, (n, 128), 0) % SLOT
+
+
+def pack(y):
+    r = row_in_slot(y.shape[0])
+    last = y[:, PACK:D]
+    out = [
+        jnp.where(r >= USED, pltpu.roll(last, USED - 4 * b, 0), y[:, 128 * b : 128 * (b + 1)])
+        for b in range(3)
+    ]
+    return jnp.concatenate(out, axis=1).astype(BF16)
+
+
+def unpack_last(y):
+    n = y.shape[0]
+    r = row_in_slot(n)
+    p = [pltpu.roll(y[:, 128 * b : 128 * (b + 1)].astype(F32), n - USED + 4 * b, 0) for b in range(3)]
+    return jnp.where(r < 4, p[0], jnp.where(r < 8, p[1], p[2])).astype(BF16)
+
+
+def chunk(ref, k):
+    return ref.at[pl.ds(pl.multiple_of(k * SLOT, SLOT), SLOT), :]
+
+
+def send_chunk(send, recv, k, target, send_sem, recv_sem):
+    pltpu.make_async_remote_copy(
+        src_ref=chunk(send, k),
+        dst_ref=chunk(recv, k),
+        send_sem=send_sem,
+        recv_sem=recv_sem,
+        device_id=device(target),
+        device_id_type=pl.DeviceIdType.MESH,
+    ).start()
+
+
+def wait_bytes(ref, sem):
+    pltpu.make_async_copy(ref, ref, sem).wait()
+
+
+def silu_parts(p):
+    sg = sigmoid(p)
+    y = p * sg
+    return y, sg + y * (1.0 - sg)
+
+
+GROUPS = 3
+ORDER = ("xyz", "yzx", "zxy")
+
+
+def step_kernel(
+    owner_ref, row_ref, stamp_row_ref, label_ref, gain_ref, head_ref, tb_ref,
+    table_hbm, first_hbm, second_hbm, w1_hbm, w2_hbm,
+    tablegrad_ref, sums_ref, usum_ref, loss_ref,
+    table_ref, first_ref, second_ref, w1_ref, w2_ref,
+    ids_send, ids_recv, idq, idrow, send, recv, back_recv, last, rows_held, hidden, slope, tok_ref,
+    normed, proj, dsl, idx, wts, dwt, att, dp, de, dpre,
+    terms, core_in, half, in1, part1, in2, u_held, u_in,
+    load_sems, sems, send_sems, recv_sems, u_sems,
 ):
+    user, item = place()
+    me = user * 16 + item
+    loads = [
+        pltpu.make_async_copy(src, dst, load_sems.at[n])
+        for n, (src, dst) in enumerate(
+            ((table_hbm, table_ref), (first_hbm, first_ref), (w1_hbm, w1_ref), (w2_hbm, w2_ref), (second_hbm, second_ref))
+        )
+    ]
+    for load in loads:
+        load.start()
+
+    def arrive(n):
+        loads[n].wait()
+
+    greet(me)
+    j_row = (UNSTEP * (owner_ref[...] - me + OWNERS)) % OWNERS
+    named = lax.broadcasted_iota(jnp.int32, (OWNERS, LOOK), 0) == j_row
+    named_b = named.astype(F32).astype(BF16)
+    before = lax.broadcasted_iota(jnp.int32, (LOOK, LOOK), 0) < lax.broadcasted_iota(
+        jnp.int32, (LOOK, LOOK), 1
+    )
+    earlier = nn(named_b, before.astype(F32).astype(BF16))
+    rank = jnp.sum(jnp.where(named, earlier, 0.0), axis=0, keepdims=True)
+    slots = j_row * SLOT + rank.astype(jnp.int32)
+    lanes = lax.broadcasted_iota(jnp.int32, (LOOK, 128), 1).astype(F32)
+    listed = jnp.where(column(rank) == lanes, column(row_ref[...]) - 256.0, 0.0)
+    ids_send[:, 0, :] = nn(named_b, listed.astype(BF16))
+    ids_recv[0] = ids_send[0]
+    meet()
+
+    @pl.loop(1, OWNERS)
+    def _(k):
+        pltpu.make_async_remote_copy(
+            src_ref=ids_send.at[k],
+            dst_ref=ids_recv.at[k],
+            send_sem=sems.at[0],
+            recv_sem=sems.at[1],
+            device_id=device((me + STEP * k) % OWNERS),
+            device_id_type=pl.DeviceIdType.MESH,
+        ).start()
+
+    slot_col = column(slots)
+    others = pl.ds(1, OWNERS - 1)
+    later = pl.ds(SLOT, ROWS - SLOT)
+    arrive(0)
+    wait_bytes(ids_recv.at[others], sems.at[1])
+    wait_bytes(ids_send.at[others], sems.at[0])
+    ids = ids_recv[:, 0, :].astype(BF16)
+
+    @pl.loop(0, ROWS // TILE)
+    def _(t):
+        base = t * TILE
+        rows = pl.ds(pl.multiple_of(base, TILE), TILE)
+        at = base + lax.broadcasted_iota(jnp.int32, (TILE, 128), 0)
+        lane = lax.broadcasted_iota(jnp.int32, (TILE, 128), 1)
+        spread = nn((at // SLOT == lane).astype(F32).astype(BF16), ids)
+        r = at % SLOT
+        mine = jnp.sum(jnp.where(r == lane, spread + 256.0, 0.0), axis=1, keepdims=True)
+        mine = jnp.where(r < USED, mine, -1.0)
+        idq[rows, :] = mine
+        cols = lane.astype(F32)
+        pick = jnp.concatenate(
+            [(mine == cols + 128.0 * b).astype(F32).astype(BF16) for b in range(4)], axis=1
+        )
+        send[rows, :] = pack(nn(pick, table_ref[...]))
+
+        @pl.loop(0, TILE // SLOT)
+        def _(i):
+            k = t * (TILE // SLOT) + i
+
+            @pl.when(k > 0)
+            def _():
+                target = (me - (STEP * k) % OWNERS + OWNERS) % OWNERS
+                send_chunk(send, recv, k, target, sems.at[2], sems.at[3])
+
+    recv[0:SLOT, :] = send[0:SLOT, :]
+    idrow[...] = idq[...].T[0:8, :]
+    arrive(1)
+    arrive(4)
+    wait_bytes(recv.at[later], sems.at[3])
+    for s in range(0, ROWS, 256):
+        rows = pl.ds(s, 256)
+        last[rows, :] = unpack_last(recv[rows, :])
+    for s in range(0, LOOK, RB):
+        rows = pl.ds(s, RB)
+        mark = slot_col[s : s + RB, :]
+        cols = lax.broadcasted_iota(jnp.int32, (RB, 128), 1).astype(F32)
+        pick = jnp.concatenate(
+            [(mark == cols + float(b)).astype(F32).astype(BF16) for b in range(0, ROWS, 128)],
+            axis=1,
+        )
+        rows_held[rows, 0:PACK] = nn(pick, recv[...]).astype(BF16)
+        rows_held[rows, PACK:D] = nn(pick, last[...]).astype(BF16)
+    for s in range(0, LOOK, 256):
+        rows = pl.ds(s, 256)
+        held = rows_held[rows, :]
+        hid, dh = silu_parts(nn(held, first_ref[...]))
+        hid = hid.astype(BF16)
+        hidden[rows, :] = hid
+        slope[rows, :] = dh
+        tok_ref[rows, :] = (held.astype(F32) + nn(hid, second_ref[...])).astype(BF16)
+    wait_bytes(send.at[later], sems.at[2])
     gain = gain_ref[...]
     head = head_ref[...]
     scale = 1.0 / math.sqrt(HD)
+    arrive(2)
     for s in range(0, LOOK, RB):
         rows = pl.ds(s, RB)
         t = tok_ref[rows, :].astype(F32)
@@ -63,10 +255,12 @@
     for k in range(BUCKETS):
         tab = tab + jnp.where(lane <= 31 - k, tb_ref[:, k : k + 1], 0.0)
     tab = jnp.where(lane == 33, NEG, tab)
+    stamp_col = column(stamp_row_ref[...]).astype(jnp.int32)
     for s in range(0, LOOK, RB):
         rows = pl.ds(s, RB)
         ke = keys_of(s)
-        gap = stamp_col_ref[rows, :] - stamp_row_ref[:, 0:ke]
+        now = jnp.concatenate([stamp_col[s : s + RB, :]] * (ke // 128), axis=1)
+        gap = now - stamp_row_ref[:, 0:ke]
         lz = lax.clz(gap + 1)
         if s < HIST:
             i_pos = s + lax.broadcasted_iota(jnp.int32, (RB, ke), 0)
@@ -112,7 +306,9 @@
     h_mid = (head - h_hi.astype(F32)).astype(BF16)
     h_lo = (head - h_hi.astype(F32) - h_mid.astype(F32)).astype(BF16)
     parts = jnp.concatenate([h_hi, h_mid, h_lo, jnp.zeros((13, D), BF16)], axis=0)
+    arrive(3)
     hw = jnp.sum(nt(parts, w2_ref[...]), axis=0, keepdims=True)
+    label_col = column(label_ref[...])
     loss = jnp.zeros((1, 1), F32)
     uvec = jnp.zeros((1, D), F32)
     dlogit = {}
@@ -126,7 +322,7 @@
         mixed = (n * g).astype(BF16).astype(F32)
         t = tok_ref[rows, :].astype(F32)
         logit = jnp.sum(t * head + mixed * hw, axis=1, keepdims=True)
-        lab = label_ref[rows, :].astype(F32)
+        lab = label_col[s : s + RB, 0:1]
         soft = jnp.maximum(logit, 0.0) + jnp.log1p(jnp.exp(-jnp.abs(logit)))
         loss = loss + jnp.sum(soft - lab * logit, axis=0, keepdims=True)
         dl = (jax.nn.sigmoid(logit) - lab) * (1.0 / LOOK)
@@ -140,7 +336,7 @@
             dn - jnp.mean(dn, axis=1, keepdims=True) - n * jnp.mean(dn * n, axis=1, keepdims=True)
         )
         att[rows, :] = da
-    uvec_ref[...] = uvec
+    u_held[0] = uvec
     loss_ref[...] = jnp.broadcast_to(loss * (1.0 / LOOK), loss_ref.shape)
     for h in range(HEADS):
         hc = h * HD
@@ -174,34 +370,247 @@
         qt = proj[:, pl.ds(2 * D + hc, HD)].astype(F32).T.astype(BF16)
         dcol = pl.ds(3 * D + hc, HD)
         dp[hist, dcol] = (nn(qt, dwt[h]).T * dsl[hist, dcol].astype(F32)).astype(BF16)
+    z, core = user // 2, user % 2
+    x, y = item // 4, item % 4
+    own = {"x": x, "y": y, "z": z}
+
+    def peer(**to):
+        c = {**own, **to}
+        return (c["z"] * 2 + to.get("core", core), c["x"] * 4 + c["y"])
+
+    def copy(src, dst, to, send_sem, recv_sem):
+        return pltpu.make_async_remote_copy(
+            src_ref=src, dst_ref=dst, send_sem=send_sem, recv_sem=recv_sem,
+            device_id=to, device_id_type=pl.DeviceIdType.MESH,
+        )
+
+    def at(n, size):
+        return pl.ds(pl.multiple_of(n * size, size), size)
+
+    def quarter(q):
+        return at(q // 4, 16), at(q % 4, 128)
+
+    def group(g):
+        return pl.ds(2 * g, 2)
+
+    def square(g):
+        a0, a1, a2 = (own[a] for a in ORDER[g])
+        rows = pl.ds(pl.multiple_of(core * 256 + a0 * 64 + a1 * 16, 16), 16)
+        return (group(g), rows, at(a2, 128))
+
+    def copies(g, stage):
+        axis, plane = ORDER[g][0], ORDER[g][1:]
+        a0 = own[axis]
+        q = own[plane[0]] * 4 + own[plane[1]]
+        todo = []
+        if stage == 0:
+            todo.append((terms.at[group(g), at(1 - core, 256), :], core_in.at[group(g)], peer(core=1 - core)))
+        elif stage == 5:
+            place_of = sums_ref.at[group(g), at(core, 256), :]
+            todo.append((place_of, place_of, peer(core=1 - core)))
+        elif stage in (1, 4):
+            for d in (1, 2, 3):
+                to = (a0 + d) % 4
+                if stage == 1:
+                    src, dst = half.at[group(g), at(to, 64), :], in1.at[g, d - 1]
+                else:
+                    src = dst = sums_ref.at[group(g), at(core * 4 + a0, 64), :]
+                todo.append((src, dst, peer(**{axis: to})))
+        else:
+            for e in range(1, 16):
+                to = (q + e) % 16
+                if stage == 2:
+                    r, c = quarter(to)
+                    src, dst = part1.at[group(g), r, c], in2.at[g, e - 1]
+                else:
+                    src = dst = sums_ref.at[square(g)]
+                todo.append((src, dst, peer(**{plane[0]: to // 4, plane[1]: to % 4})))
+        return [
+            copy(src, dst, to, send_sems.at[g, stage, n], recv_sems.at[g, stage, n])
+            for n, (src, dst, to) in enumerate(todo)
+        ]
+
+    def start(g, stage):
+        for c in copies(g, stage):
+            c.start()
+
+    def finish(g, stage):
+        for c in copies(g, stage):
+            c.wait_recv()
+        a0, a1, a2 = (own[a] for a in ORDER[g])
+        if stage == 0:
+            for b in (2 * g, 2 * g + 1):
+                half[b] = (terms[b, at(core, 256), :].astype(F32) + core_in[b].astype(F32)).astype(BF16)
+        elif stage == 1:
+            total = half[group(g), at(a0, 64), :].astype(F32)
+            for d in range(3):
+                total = total + in1[g, d].astype(F32)
+            part1[group(g)] = total.astype(BF16)
+        elif stage == 2:
+            total = part1[group(g), at(a1, 16), at(a2, 128)].astype(F32)
+            for e in range(15):
+                total = total + in2[g, e].astype(F32)
+            sums_ref[square(g)] = total.astype(BF16)
+
+    def u_copies(stage):
+        if stage == 0:
+            peers = [peer(core=1 - core)]
+        else:
+            a = "xyz"[stage - 1]
+            peers = [peer(**{a: (own[a] + d) % 4}) for d in (1, 2, 3)]
+        return [
+            copy(u_held.at[stage], u_in.at[stage, n], to, u_sems.at[0, stage, n], u_sems.at[1, stage, n])
+            for n, to in enumerate(peers)
+        ]
+
+    def u_start(stage):
+        for c in u_copies(stage):
+            c.start()
+
+    def u_finish(stage):
+        total = u_held[stage]
+        for n, c in enumerate(u_copies(stage)):
+            c.wait_recv()
+            total = total + u_in[stage, n]
+        if stage < 3:
+            u_held[stage + 1] = total
+        else:
+            usum_ref[...] = total
+
+    u_start(0)
+    nrt = normed[...].astype(F32).T.astype(BF16)
+    for b in range(4):
+        for c in range(0, D, 256):
+            terms[b, :, pl.ds(c, 256)] = nn(nrt, dp[:, pl.ds(b * D + c, 256)]).astype(BF16)
+        if b % 2:
+            start(b // 2, 0)
     for s in range(0, LOOK, RB):
         rows = pl.ds(s, RB)
         dnorm = nt(dp[rows, :], w1_ref[...])
         t = tok_ref[rows, :].astype(F32)
         r = lax.rsqrt(jnp.mean(t * t, axis=1, keepdims=True) + EPS)
         tn = dnorm * gain
-        tgrad_ref[rows, :] = (
-            dlogit[s] * head + r * tn - t * (r * r * r * jnp.mean(tn * t, axis=1, keepdims=True))
-        ).astype(BF16)
-    nrt = normed[...].astype(F32).T.astype(BF16)
-    for c in range(0, 4 * D, 256):
-        cols = pl.ds(c, 256)
-        iterm_ref[:, cols] = nn(nrt, dp[:, cols]).astype(BF16)
-
-
-def hstu(tok, w1, w2, gain, head, tb, stamps, labels):
-    vm = pl.BlockSpec(memory_space=pltpu.VMEM)
+        tg = dlogit[s] * head + r * tn - t * (r * r * r * jnp.mean(tn * t, axis=1, keepdims=True))
+        tgb = tg.astype(BF16)
+        de[rows, :] = tgb
+        dpr = (nt(tgb, second_ref[...]) * slope[rows, :]).astype(BF16)
+        dpre[rows, :] = dpr
+        att[rows, :] = tg + nt(dpr, first_ref[...])
+    for g in (0, 1):
+        finish(g, 0)
+        start(g, 1)
+    u_finish(0)
+    u_start(1)
+    row_grad = att[...].astype(BF16)
+
+    @pl.loop(0, ROWS // TILE)
+    def _(t):
+        base = t * TILE
+        rows = pl.ds(pl.multiple_of(base, TILE), TILE)
+        pick = base + lax.broadcasted_iota(jnp.int32, (TILE, LOOK), 0) == slots
+        send[rows, :] = pack(nn(pick.astype(F32).astype(BF16), row_grad))
+
+        @pl.loop(0, TILE // SLOT)
+        def _(i):
+            k = t * (TILE // SLOT) + i
+
+            @pl.when(k > 0)
+            def _():
+                send_chunk(send, back_recv, k, (me + STEP * k) % OWNERS, sems.at[4], sems.at[5])
+
+    back_recv[0:SLOT, :] = send[0:SLOT, :]
+    terms[5] = nn(hidden[...].astype(F32).T.astype(BF16), de[...]).astype(BF16)
+    terms[4] = nn(rows_held[...].astype(F32).T.astype(BF16), dpre[...]).astype(BF16)
+    start(2, 0)
+    for g in (0, 1):
+        finish(g, 1)
+        start(g, 2)
+    u_finish(1)
+    u_start(2)
+    finish(2, 0)
+    start(2, 1)
+    for g in (0, 1):
+        finish(g, 2)
+        start(g, 3)
+    u_finish(2)
+    u_start(3)
+    finish(2, 1)
+    start(2, 2)
+    for g in (0, 1):
+        finish(g, 3)
+        start(g, 4)
+    finish(2, 2)
+    start(2, 3)
+    u_finish(3)
+    wait_bytes(back_recv.at[later], sems.at[5])
+    for s in range(0, ROWS, 256):
+        rows = pl.ds(s, 256)
+        last[rows, :] = unpack_last(back_recv[rows, :])
+    for s in range(0, D, 128):
+        rows = pl.ds(s, 128)
+        sub = (s + lax.broadcasted_iota(jnp.int32, (128, 128), 0)).astype(F32)
+        pick = jnp.concatenate(
+            [
+                (sub == idrow[0:1, q : q + 128]).astype(F32).astype(BF16)
+                for q in range(0, ROWS, 128)
+            ],
+            axis=1,
+        )
+        tablegrad_ref[rows, 0:PACK] = nn(pick, back_recv[...])
+        tablegrad_ref[rows, PACK:D] = nn(pick, last[...])
+    finish(2, 3)
+    start(2, 4)
+    for g in (0, 1):
+        finish(g, 4)
+        start(g, 5)
+    finish(2, 4)
+    start(2, 5)
+    for g in range(GROUPS):
+        finish(g, 5)
+    wait_bytes(send.at[later], sems.at[4])
+    for stage in range(4):
+        for c in u_copies(stage):
+            c.wait_send()
+    for g in range(GROUPS):
+        for stage in range(6):
+            for c in copies(g, stage):
+                c.wait_send()
+
+
+VM = pl.BlockSpec(memory_space=pltpu.VMEM)
+ANY = pl.BlockSpec(memory_space=pl.ANY)
+
+
+def train_step(*args):
+    dma = pltpu.SemaphoreType.DMA
     return pl.pallas_call(
-        hstu_kernel,
+        step_kernel,
         out_shape=(
-            jax.ShapeDtypeStruct((LOOK, D), BF16),
-            jax.ShapeDtypeStruct((D, 4 * D), BF16),
+            jax.ShapeDtypeStruct((D, D), F32),
+            jax.ShapeDtypeStruct((2 * GROUPS, D, D), BF16),
             jax.ShapeDtypeStruct((1, D), F32),
             jax.ShapeDtypeStruct((1, 128), F32),
         ),
-        in_specs=[vm] * 9,
-        out_specs=(vm,) * 4,
+        in_specs=[VM] * 7 + [ANY] * 5,
+        out_specs=(VM,) * 4,
         scratch_shapes=[
+            pltpu.VMEM((D, D), BF16),
+            pltpu.VMEM((D, D), BF16),
+            pltpu.VMEM((D, D), BF16),
+            pltpu.VMEM((D, 4 * D), BF16),
+            pltpu.VMEM((D, D), BF16),
+            pltpu.VMEM((OWNERS, 1, 128), F32),
+            pltpu.VMEM((OWNERS, 1, 128), F32),
+            pltpu.VMEM((ROWS, 128), F32),
+            pltpu.VMEM((8, ROWS), F32),
+            pltpu.VMEM((ROWS, PACK), BF16),
+            pltpu.VMEM((ROWS, PACK), BF16),
+            pltpu.VMEM((ROWS, PACK), BF16),
+            pltpu.VMEM((ROWS, 128), BF16),
+            pltpu.VMEM((LOOK, D), BF16),
+            pltpu.VMEM((LOOK, D), BF16),
+            pltpu.VMEM((LOOK, D), F32),
+            pltpu.VMEM((LOOK, D), BF16),
             pltpu.VMEM((LOOK, D), BF16),
             pltpu.VMEM((LOOK, 4 * D), BF16),
             pltpu.VMEM((LOOK, 4 * D), BF16),
@@ -210,74 +619,76 @@
             pltpu.VMEM((HEADS, LOOK, HIST), BF16),
             pltpu.VMEM((LOOK, D), F32),
             pltpu.VMEM((LOOK, 4 * D), BF16),
-            pltpu.VMEM((8, 128), F32),
+            pltpu.VMEM((LOOK, D), BF16),
+            pltpu.VMEM((LOOK, D), BF16),
+            pltpu.VMEM((2 * GROUPS, D, D), BF16),
+            pltpu.VMEM((2 * GROUPS, 256, D), BF16),
+            pltpu.VMEM((2 * GROUPS, 256, D), BF16),
+            pltpu.VMEM((GROUPS, 3, 2, 64, D), BF16),
+            pltpu.VMEM((2 * GROUPS, 64, D), BF16),
+            pltpu.VMEM((GROUPS, 15, 2, 16, 128), BF16),
+            pltpu.VMEM((4, 1, D), F32),
+            pltpu.VMEM((4, 3, 1, D), F32),
+            dma((5,)),
+            dma((6,)),
+            dma((GROUPS, 6, 15)),
+            dma((GROUPS, 6, 15)),
+            dma((2, 4, 3)),
         ],
-        compiler_params=pltpu.CompilerParams(vmem_limit_bytes=56 * 2**20),
-        cost_estimate=pl.CostEstimate(flops=8 * 10**9, bytes_accessed=8 * 2**20, transcendentals=4 * 10**6),
-        name="hstu",
-    )(
-        tok, w1, w2, gain.reshape(1, D), head.reshape(1, D), tb,
-        stamps.reshape(1, LOOK), stamps.reshape(LOOK, 1), labels.reshape(LOOK, 1),
-    )
-
-
-def tower_block(item_rows, first, second):
-    hidden_items = jax.nn.silu(
-        jnp.dot(item_rows.astype(jnp.bfloat16), first, preferred_element_type=jnp.float32)
-    ).astype(jnp.bfloat16)
-    return item_rows + jnp.dot(hidden_items, second, preferred_element_type=jnp.float32)
+        compiler_params=pltpu.CompilerParams(
+            vmem_limit_bytes=60 * 2**20, collective_id=0, has_side_effects=True
+        ),
+        cost_estimate=pl.CostEstimate(
+            flops=14 * 10**9, bytes_accessed=10 * 2**20, transcendentals=5 * 10**6
+        ),
+        name="step",
+    )(*args)
+
+
+def finish_kernel(tablegrad_ref, sums_ref, usum_ref, head_ref, table_ref, first_ref, second_ref, input_ref, output_ref):
+    table_ref[...] = tablegrad_ref[...]
+    first_ref[...] = sums_ref[4].astype(F32)
+    second_ref[...] = sums_ref[5].astype(F32)
+    for b in range(4):
+        input_ref[:, pl.ds(b * D, D)] = sums_ref[b].astype(F32)
+    output_ref[...] = column(usum_ref[...])[:, 0:1] * head_ref[...]
+
+
+def outputs(tablegrad, sums, usum, head):
+    n = 128
+
+    def rows(width):
+        return pl.BlockSpec((n, width), lambda i: (i, 0))
+
+    def shape(width):
+        return jax.ShapeDtypeStruct((D, width), F32)
+
+    return pl.pallas_call(
+        finish_kernel,
+        grid=(D // n,),
+        out_shape=(shape(D), shape(D), shape(D), shape(4 * D), shape(D)),
+        in_specs=[
+            rows(D),
+            pl.BlockSpec((2 * GROUPS, n, D), lambda i: (0, i, 0)),
+            pl.BlockSpec((1, n), lambda i: (0, i)),
+            pl.BlockSpec((1, D), lambda i: (0, 0)),
+        ],
+        out_specs=(rows(D), rows(D), rows(D), rows(4 * D), rows(D)),
+        compiler_params=pltpu.CompilerParams(vmem_limit_bytes=60 * 2**20),
+        name="outputs",
+    )(tablegrad, sums, usum, head)
 
 
 def body(
     table, tower_first, tower_second, w_input, w_output, norm_gain, head_vec, time_bias,
     look_owner, look_row, event_time, labels,
 ):
-    n_user = lax.axis_size("user")
-    n_item = lax.axis_size("item")
-    owners = n_user * n_item
-    lookups = look_row.shape[1]
-    features = table.shape[1]
-    capacity = 12
-    owner_ids = look_owner[0, :, 0]
-    targets = jnp.arange(owners, dtype=jnp.int32)
-    onehot = (owner_ids[:, None] == targets[None, :]).astype(jnp.int32)
-    position = jnp.sum(onehot * (jnp.cumsum(onehot, axis=0) - 1), axis=1)
-    slot_index = owner_ids * capacity + position
-    send_ids = (
-        jnp.full((owners * capacity,), -1, jnp.int32)
-        .at[slot_index]
-        .set(look_row[0])
-        .reshape(owners, capacity)
+    head = head_vec.reshape(1, D)
+    tablegrad, sums, usum, loss = train_step(
+        look_owner.reshape(1, LOOK), look_row, event_time, labels, norm_gain.reshape(1, D), head,
+        time_bias, table, tower_first, tower_second, w_input, w_output,
     )
-    recv_ids = lax.all_to_all(send_ids, ("user", "item"), split_axis=0, concat_axis=0, tiled=True)
-    item_rows = table.astype(jnp.float32)
-    embed_f, tower_back = jax.vjp(tower_block, item_rows, tower_first, tower_second)
-    embedding = embed_f.astype(jnp.bfloat16)
-    is_live = recv_ids >= 0
-    safe_rows = jnp.where(is_live, recv_ids, 0)
-    replies = jnp.where(is_live[:, :, None], embedding[safe_rows], jnp.zeros((), jnp.bfloat16))
-    back_rows = lax.all_to_all(replies, ("user", "item"), split_axis=0, concat_axis=0, tiled=True)
-    tok = back_rows.reshape(owners * capacity, features)[slot_index]
-    token_grad, input_term, uvec, loss = hstu(
-        tok, w_input, w_output, norm_gain, head_vec, time_bias, event_time, labels
-    )
-    send_grad = (
-        jnp.zeros((owners * capacity, features), BF16)
-        .at[slot_index]
-        .set(token_grad)
-        .reshape(owners, capacity, features)
-    )
-    input_grad, uvec = lax.psum((input_term.astype(F32), uvec[0]), ("user", "item"))
-    output_grad = uvec[:, None] * head_vec[None, :]
-    recv_grad = lax.all_to_all(
-        send_grad, ("user", "item"), split_axis=0, concat_axis=0, tiled=True
-    ).astype(F32)
-    live_grad = jnp.where(is_live[:, :, None], recv_grad, 0.0).reshape(owners * capacity, features)
-    embed_grad = jnp.zeros_like(item_rows).at[safe_rows.reshape(-1)].add(live_grad)
-    table_grad, first_term, second_term = tower_back(embed_grad)
-    first_grad, second_grad = lax.psum(
-        (first_term.astype(F32), second_term.astype(F32)), ("user", "item")
-    )
+    table_grad, first_grad, second_grad, input_grad, output_grad = outputs(tablegrad, sums, usum, head)
     return (table_grad, first_grad, second_grad, input_grad, output_grad, loss[0, :1])
 
 

time: 337 us -> 142 us (0.42); the launches traced: 332 us -> 142 us
  Pallas kernels: 23.2 us -> 140 us
  waiting for transfers between devices: 105 us -> 0 us
  blocking collectives: 104 us -> 0 us
  local copies, waits for them, and re-layouts: 36.5 us -> 0.01 us
  starting transfers between devices: 21.6 us -> 0 us
  other arithmetic: 19.8 us -> 0 us
  between operations: 14.6 us -> 1.82 us
  matrix products: 7.21 us -> 0 us
    pallas_call x1 -> x2, Pallas kernels: 23.2 us -> 140 us  [the longest x1 134 us: train_step(): pl.pallas_call(step_kernel, out_shape=(jax.ShapeDtypeStruct((D, D), F32),...]
    psum x1 -> x0, blocking collectives: 104 us -> none  [body(): lax.psum((input_term.astype(F32), uvec[0]), ('user', 'item'))]
    all_to_all x3 -> x0, waiting for transfers between devices: 64 us -> none  [the longest x1 28.3 us: body(): lax.all_to_all(send_grad, ('user', 'item'), split_axis=0, concat_axis=0,...]
    psum x1 -> x0, waiting for transfers between devices: 41.3 us -> none  [body(): lax.psum((first_term.astype(F32), second_term.astype(F32)), ('user', 'ite...]
    all_to_all x3 -> x0, starting transfers between devices: 21.6 us -> none  [the longest x1 11.5 us: body(): lax.all_to_all(send_ids, ('user', 'item'), split_axis=0, concat_axis=0, t...]
    scatter-add x1 -> x0, other arithmetic: 10.5 us -> none  [body(): jnp.zeros_like(item_rows).at[safe_rows.reshape(-1)].add(live_grad)]
    reshape x5 -> x0, local copies, waits for them, and re-layouts: 10.5 us -> none  [the longest x1 4.61 us: body(): jnp.where(is_live[:, :, None], recv_grad, 0.0)]
    gather x3 -> x0, local copies, waits for them, and re-layouts: 10.1 us -> none  [the longest x2 6.32 us: body(): embedding[safe_rows]]
  transfers between devices with their start and end apart: 4 -> 0, of which waited for: 4 -> 0; matrix products, arithmetic and copies ran while one was open for 2% -> 0% of each run, Pallas kernels for 0% -> 0%
where the time goes in v3:
time: 142 us
  Pallas kernels  140 us (99%)
  between operations  1.82 us (1%)
    pallas_call x1, Pallas kernels, train_step(): pl.pallas_call(step_kernel, out_shape=(jax.ShapeDtypeStruct((D, D), F32),...  134 us
    pallas_call x1, Pallas kernels, outputs(): pl.pallas_call(finish_kernel, grid=(D // n,), out_shape=(shape(D), shape(...  5.86 us

profile of v3, /device:TPU:1, one launch (start us, length us, event | category | flops | bytes accessed | tf_op | source)
XLA Modules:
  0.0 141.5 jit_solution(6047222614862578644)
XLA Ops:
  0.6 133.8 %step.1 = (f32[512,512]{1,0:T(8,128)}, bf16[6,512,512]{2,1,0:T(8,128)(2,1)}, f32[1,512]{1,0:T(1,128)}, f32[1,128]{1,0:T(1,128)}) custom-call(s32[1,768]{1,0:T(1,128)} %bitcast.7, s32[1,768]{1,0:T(1,128)} %row_ref.1, s32[1,768]{1,0:T(1,128)} %stamp_row_ref.1, s32[1,768]{1,0:T(1,128)} %label_ref.1, f32[1,512]{1,0:T(1,128)} %bitcast.8, f32[1,512]{1,0:T(1,128)} %bitcast.5, ...), custom_call_target="tpu_custom_call" | custom-call | flops 14000000000 | bytes 10485760 | tf_op jit(solution)/shard_map/step/pallas_call | solution.py:586
  134.5 0.0 copy-start
  134.5 5.9 %outputs.1 = (f32[512,512]{1,0:T(8,128)}, f32[512,512]{1,0:T(8,128)}, f32[512,512]{1,0:T(8,128)}, f32[512,2048]{1,0:T(8,128)}, f32[512,512]{1,0:T(8,128)}) custom-call(f32[512,512]{1,0:T(8,128)} %get-tuple-element.15.tablegrad_ref, bf16[6,512,512]{2,1,0:T(8,128)(2,1)} %get-tuple-element.16.sums_ref, f32[1,512]{1,0:T(1,128)} %get-tuple-element.17.usum_ref, ...), custom_call_target="tpu_custom_call" | custom-call | tf_op jit(solution)/shard_map/outputs/pallas_call | solution.py:666
  140.4 0.0 copy-done
Async XLA Ops:
  134.5 5.9 %copy-start = (f32[1,128]{1,0:T(1,128)S(1)}, f32[1,128]{1,0:T(1,128)}, u32[]{:S(2)}) copy-start(f32[1,128]{1,0:T(1,128)} %get-tuple-element.23) | copy-start | bytes 1540

commit v4 on v3

--- a/solution.py
+++ b/solution.py
@@ -56,14 +56,22 @@
     return (index // 16, index % 16)
 
 
-def greet(me):
+def greet():
     barrier = pltpu.get_barrier_semaphore()
 
-    @pl.loop(1, OWNERS)
-    def _(k):
-        pl.semaphore_signal(
-            barrier, inc=1, device_id=device((me + k) % OWNERS), device_id_type=pl.DeviceIdType.MESH
-        )
+    user, item = place()
+
+    def hail(du, di):
+        to = ((user + du) % 8, (item + di) % 16)
+        pl.semaphore_signal(barrier, inc=1, device_id=to, device_id_type=pl.DeviceIdType.MESH)
+
+    for di in range(1, 16):
+        hail(0, di)
+    for di in range(16):
+
+        @pl.loop(1, 8)
+        def _(du):
+            hail(du, di)
 
 
 def meet():
@@ -123,12 +131,12 @@
 def step_kernel(
     owner_ref, row_ref, stamp_row_ref, label_ref, gain_ref, head_ref, tb_ref,
     table_hbm, first_hbm, second_hbm, w1_hbm, w2_hbm,
-    tablegrad_ref, sums_ref, usum_ref, loss_ref,
-    table_ref, first_ref, second_ref, w1_ref, w2_ref,
+    tablegrad_hbm, sums_hbm, usum_ref, loss_ref,
+    sums_ref, table_ref, first_ref, second_ref, w1_ref, w2_ref,
     ids_send, ids_recv, idq, idrow, send, recv, back_recv, last, rows_held, hidden, slope, tok_ref,
     normed, proj, dsl, idx, wts, dwt, att, dp, de, dpre,
     terms, core_in, half, in1, part1, in2, u_held, u_in,
-    load_sems, sems, send_sems, recv_sems, u_sems,
+    load_sems, out_sems, sems, send_sems, recv_sems, u_sems,
 ):
     user, item = place()
     me = user * 16 + item
@@ -144,7 +152,7 @@
     def arrive(n):
         loads[n].wait()
 
-    greet(me)
+    greet()
     j_row = (UNSTEP * (owner_ref[...] - me + OWNERS)) % OWNERS
     named = lax.broadcasted_iota(jnp.int32, (OWNERS, LOOK), 0) == j_row
     named_b = named.astype(F32).astype(BF16)
@@ -179,14 +187,16 @@
     wait_bytes(ids_send.at[others], sems.at[0])
     ids = ids_recv[:, 0, :].astype(BF16)
 
-    @pl.loop(0, ROWS // TILE)
-    def _(t):
+    def fresh(t):
+        return max(1, t * (TILE // SLOT)), (t + 1) * (TILE // SLOT)
+
+    for t in range(ROWS // TILE):
         base = t * TILE
-        rows = pl.ds(pl.multiple_of(base, TILE), TILE)
-        at = base + lax.broadcasted_iota(jnp.int32, (TILE, 128), 0)
+        rows = pl.ds(base, TILE)
+        slot_at = base + lax.broadcasted_iota(jnp.int32, (TILE, 128), 0)
         lane = lax.broadcasted_iota(jnp.int32, (TILE, 128), 1)
-        spread = nn((at // SLOT == lane).astype(F32).astype(BF16), ids)
-        r = at % SLOT
+        spread = nn((slot_at // SLOT == lane).astype(F32).astype(BF16), ids)
+        r = slot_at % SLOT
         mine = jnp.sum(jnp.where(r == lane, spread + 256.0, 0.0), axis=1, keepdims=True)
         mine = jnp.where(r < USED, mine, -1.0)
         idq[rows, :] = mine
@@ -196,33 +206,28 @@
         )
         send[rows, :] = pack(nn(pick, table_ref[...]))
 
-        @pl.loop(0, TILE // SLOT)
-        def _(i):
-            k = t * (TILE // SLOT) + i
-
-            @pl.when(k > 0)
-            def _():
-                target = (me - (STEP * k) % OWNERS + OWNERS) % OWNERS
-                send_chunk(send, recv, k, target, sems.at[2], sems.at[3])
+        @pl.loop(*fresh(t))
+        def _(k):
+            target = (me - (STEP * k) % OWNERS + OWNERS) % OWNERS
+            send_chunk(send, recv, k, target, sems.at[2], sems.at[3])
 
     recv[0:SLOT, :] = send[0:SLOT, :]
     idrow[...] = idq[...].T[0:8, :]
+    for s in range(0, LOOK, RB):
+        mark = slot_col[s : s + RB, :]
+        cols = lax.broadcasted_iota(jnp.int32, (RB, 128), 1).astype(F32)
+        for b in range(0, ROWS, 128):
+            dp[pl.ds(s, RB), pl.ds(b, 128)] = (mark == cols + float(b)).astype(F32).astype(BF16)
     arrive(1)
     arrive(4)
     wait_bytes(recv.at[later], sems.at[3])
     for s in range(0, ROWS, 256):
         rows = pl.ds(s, 256)
         last[rows, :] = unpack_last(recv[rows, :])
-    for s in range(0, LOOK, RB):
-        rows = pl.ds(s, RB)
-        mark = slot_col[s : s + RB, :]
-        cols = lax.broadcasted_iota(jnp.int32, (RB, 128), 1).astype(F32)
-        pick = jnp.concatenate(
-            [(mark == cols + float(b)).astype(F32).astype(BF16) for b in range(0, ROWS, 128)],
-            axis=1,
-        )
-        rows_held[rows, 0:PACK] = nn(pick, recv[...]).astype(BF16)
-        rows_held[rows, PACK:D] = nn(pick, last[...]).astype(BF16)
+    for s in range(0, LOOK, 256):
+        rows = pl.ds(s, 256)
+        rows_held[rows, 0:PACK] = nn(dp[rows, :], recv[...]).astype(BF16)
+        rows_held[rows, PACK:D] = nn(dp[rows, :], last[...]).astype(BF16)
     for s in range(0, LOOK, 256):
         rows = pl.ds(s, 256)
         held = rows_held[rows, :]
@@ -406,8 +411,8 @@
         if stage == 0:
             todo.append((terms.at[group(g), at(1 - core, 256), :], core_in.at[group(g)], peer(core=1 - core)))
         elif stage == 5:
-            place_of = sums_ref.at[group(g), at(core, 256), :]
-            todo.append((place_of, place_of, peer(core=1 - core)))
+            half_of = (group(g), at(core, 256))
+            todo.append((sums_ref.at[half_of], sums_hbm.at[half_of], peer(core=1 - core)))
         elif stage in (1, 4):
             for d in (1, 2, 3):
                 to = (a0 + d) % 4
@@ -430,9 +435,15 @@
             for n, (src, dst, to) in enumerate(todo)
         ]
 
+    def own_half(g):
+        half_of = (group(g), at(core, 256))
+        return pltpu.make_async_copy(sums_ref.at[half_of], sums_hbm.at[half_of], out_sems.at[g])
+
     def start(g, stage):
         for c in copies(g, stage):
             c.start()
+        if stage == 5:
+            own_half(g).start()
 
     def finish(g, stage):
         for c in copies(g, stage):
@@ -496,6 +507,9 @@
         dpr = (nt(tgb, second_ref[...]) * slope[rows, :]).astype(BF16)
         dpre[rows, :] = dpr
         att[rows, :] = tg + nt(dpr, first_ref[...])
+    terms[5] = nn(hidden[...].astype(F32).T.astype(BF16), de[...]).astype(BF16)
+    terms[4] = nn(rows_held[...].astype(F32).T.astype(BF16), dpre[...]).astype(BF16)
+    start(2, 0)
     for g in (0, 1):
         finish(g, 0)
         start(g, 1)
@@ -503,70 +517,57 @@
     u_start(1)
     row_grad = att[...].astype(BF16)
 
-    @pl.loop(0, ROWS // TILE)
-    def _(t):
+    for t in range(ROWS // TILE):
         base = t * TILE
-        rows = pl.ds(pl.multiple_of(base, TILE), TILE)
+        rows = pl.ds(base, TILE)
         pick = base + lax.broadcasted_iota(jnp.int32, (TILE, LOOK), 0) == slots
         send[rows, :] = pack(nn(pick.astype(F32).astype(BF16), row_grad))
 
-        @pl.loop(0, TILE // SLOT)
-        def _(i):
-            k = t * (TILE // SLOT) + i
-
-            @pl.when(k > 0)
-            def _():
-                send_chunk(send, back_recv, k, (me + STEP * k) % OWNERS, sems.at[4], sems.at[5])
-
+        @pl.loop(*fresh(t))
+        def _(k):
+            send_chunk(send, back_recv, k, (me + STEP * k) % OWNERS, sems.at[4], sems.at[5])
+
+        if t == 0:
+            finish(2, 0)
+            start(2, 1)
     back_recv[0:SLOT, :] = send[0:SLOT, :]
-    terms[5] = nn(hidden[...].astype(F32).T.astype(BF16), de[...]).astype(BF16)
-    terms[4] = nn(rows_held[...].astype(F32).T.astype(BF16), dpre[...]).astype(BF16)
-    start(2, 0)
     for g in (0, 1):
         finish(g, 1)
         start(g, 2)
     u_finish(1)
     u_start(2)
-    finish(2, 0)
-    start(2, 1)
-    for g in (0, 1):
-        finish(g, 2)
-        start(g, 3)
-    u_finish(2)
-    u_start(3)
     finish(2, 1)
     start(2, 2)
-    for g in (0, 1):
-        finish(g, 3)
-        start(g, 4)
-    finish(2, 2)
-    start(2, 3)
-    u_finish(3)
+    for s in range(0, D, 128):
+        sub = (s + lax.broadcasted_iota(jnp.int32, (128, 128), 0)).astype(F32)
+        for q in range(0, ROWS, 128):
+            proj[pl.ds(s, 128), pl.ds(q, 128)] = (
+                (sub == idrow[0:1, q : q + 128]).astype(F32).astype(BF16)
+            )
+    for stage in (2, 3):
+        for g in range(GROUPS):
+            finish(g, stage)
+            start(g, stage + 1)
+        u_finish(stage)
+        if stage == 2:
+            u_start(3)
     wait_bytes(back_recv.at[later], sems.at[5])
     for s in range(0, ROWS, 256):
         rows = pl.ds(s, 256)
         last[rows, :] = unpack_last(back_recv[rows, :])
-    for s in range(0, D, 128):
-        rows = pl.ds(s, 128)
-        sub = (s + lax.broadcasted_iota(jnp.int32, (128, 128), 0)).astype(F32)
-        pick = jnp.concatenate(
-            [
-                (sub == idrow[0:1, q : q + 128]).astype(F32).astype(BF16)
-                for q in range(0, ROWS, 128)
-            ],
-            axis=1,
-        )
-        tablegrad_ref[rows, 0:PACK] = nn(pick, back_recv[...])
-        tablegrad_ref[rows, PACK:D] = nn(pick, last[...])
-    finish(2, 3)
-    start(2, 4)
-    for g in (0, 1):
+    for s in range(0, D, 256):
+        rows = pl.ds(s, 256)
+        att[rows, 0:PACK] = nn(proj[rows, :], back_recv[...])
+        att[rows, PACK:D] = nn(proj[rows, :], last[...])
+    table_out = pltpu.make_async_copy(att.at[pl.ds(0, D), :], tablegrad_hbm, out_sems.at[3])
+    table_out.start()
+    for g in range(GROUPS):
         finish(g, 4)
         start(g, 5)
-    finish(2, 4)
-    start(2, 5)
     for g in range(GROUPS):
         finish(g, 5)
+        own_half(g).wait()
+    table_out.wait()
     wait_bytes(send.at[later], sems.at[4])
     for stage in range(4):
         for c in u_copies(stage):
@@ -592,8 +593,9 @@
             jax.ShapeDtypeStruct((1, 128), F32),
         ),
         in_specs=[VM] * 7 + [ANY] * 5,
-        out_specs=(VM,) * 4,
+        out_specs=(ANY, ANY, VM, VM),
         scratch_shapes=[
+            pltpu.VMEM((2 * GROUPS, D, D), BF16),
             pltpu.VMEM((D, D), BF16),
             pltpu.VMEM((D, D), BF16),
             pltpu.VMEM((D, D), BF16),
@@ -630,6 +632,7 @@
             pltpu.VMEM((4, 1, D), F32),
             pltpu.VMEM((4, 3, 1, D), F32),
             dma((5,)),
+            dma((4,)),
             dma((6,)),
             dma((GROUPS, 6, 15)),
             dma((GROUPS, 6, 15)),

time: 142 us -> 134 us (0.944)
  Pallas kernels: 140 us -> 132 us
    pallas_call x1, Pallas kernels: 134 us -> 126 us  [train_step(): pl.pallas_call(step_kernel, out_shape=(jax.ShapeDtypeStruct((D, D), F32),...]
where the time goes in v4:
time: 134 us
  Pallas kernels  132 us (99%)
  between operations  1.82 us (1%)
    pallas_call x1, Pallas kernels, train_step(): pl.pallas_call(step_kernel, out_shape=(jax.ShapeDtypeStruct((D, D), F32),...  126 us
    pallas_call x1, Pallas kernels, outputs(): pl.pallas_call(finish_kernel, grid=(D // n,), out_shape=(shape(D), shape(...  5.86 us

profile of v4, /device:TPU:1, one launch (start us, length us, event | category | flops | bytes accessed | tf_op | source)
XLA Modules:
  0.0 133.6 jit_solution(3318715362199742783)
XLA Ops:
  0.6 125.9 %step.1 = (f32[512,512]{1,0:T(8,128)}, bf16[6,512,512]{2,1,0:T(8,128)(2,1)}, f32[1,512]{1,0:T(1,128)}, f32[1,128]{1,0:T(1,128)}) custom-call(s32[1,768]{1,0:T(1,128)} %bitcast.7, s32[1,768]{1,0:T(1,128)} %row_ref.1, s32[1,768]{1,0:T(1,128)} %stamp_row_ref.1, s32[1,768]{1,0:T(1,128)} %label_ref.1, f32[1,512]{1,0:T(1,128)} %bitcast.8, f32[1,512]{1,0:T(1,128)} %bitcast.5, ...), custom_call_target="tpu_custom_call" | custom-call | flops 14000000000 | bytes 10485760 | tf_op jit(solution)/shard_map/step/pallas_call | solution.py:587
  126.6 0.0 copy-start
  126.6 5.9 %outputs.1 = (f32[512,512]{1,0:T(8,128)}, f32[512,512]{1,0:T(8,128)}, f32[512,512]{1,0:T(8,128)}, f32[512,2048]{1,0:T(8,128)}, f32[512,512]{1,0:T(8,128)}) custom-call(f32[512,512]{1,0:T(8,128)} %get-tuple-element.15.tablegrad_ref, bf16[6,512,512]{2,1,0:T(8,128)(2,1)} %get-tuple-element.16.sums_ref, f32[1,512]{1,0:T(1,128)} %get-tuple-element.17.usum_ref, ...), custom_call_target="tpu_custom_call" | custom-call | tf_op jit(solution)/shard_map/outputs/pallas_call | solution.py:669
  132.4 0.0 copy-done
Async XLA Ops:
  126.6 5.9 %copy-start = (f32[1,128]{1,0:T(1,128)S(1)}, f32[1,128]{1,0:T(1,128)}, u32[]{:S(2)}) copy-start(f32[1,128]{1,0:T(1,128)} %get-tuple-element.23) | copy-start | bytes 1540

commit v5 on v4

--- a/solution.py
+++ b/solution.py
@@ -126,6 +126,11 @@
 
 GROUPS = 3
 ORDER = ("xyz", "yzx", "zxy")
+BATCH = 8
+PLAN = {
+    0: (2, 0), 3: (0, 1), 4: (1, 1), 5: (2, 1), 6: (0, 2), 7: (1, 2), 8: (2, 2),
+    9: (0, 3), 10: (1, 3), 11: (2, 3), 14: (0, 4), 15: (1, 4),
+}
 
 
 def step_kernel(
@@ -149,6 +154,9 @@
     for load in loads:
         load.start()
 
+    gain = gain_ref[...]
+    head = head_ref[...]
+
     def arrive(n):
         loads[n].wait()
 
@@ -218,6 +226,29 @@
         cols = lax.broadcasted_iota(jnp.int32, (RB, 128), 1).astype(F32)
         for b in range(0, ROWS, 128):
             dp[pl.ds(s, RB), pl.ds(b, 128)] = (mark == cols + float(b)).astype(F32).astype(BF16)
+    lane = lax.broadcasted_iota(jnp.int32, (HEADS, 128), 1)
+    tab = jnp.zeros((HEADS, 128), F32)
+    for k in range(BUCKETS):
+        tab = tab + jnp.where(lane <= 31 - k, tb_ref[:, k : k + 1], 0.0)
+    tab = jnp.where(lane == 33, NEG, tab)
+    stamp_col = column(stamp_row_ref[...]).astype(jnp.int32)
+    for s in range(0, LOOK, RB):
+        rows = pl.ds(s, RB)
+        ke = keys_of(s)
+        now = jnp.concatenate([stamp_col[s : s + RB, :]] * (ke // 128), axis=1)
+        gap = now - stamp_row_ref[:, 0:ke]
+        lz = lax.clz(gap + 1)
+        if s < HIST:
+            i_pos = s + lax.broadcasted_iota(jnp.int32, (RB, ke), 0)
+            j_pos = lax.broadcasted_iota(jnp.int32, (RB, ke), 1)
+            lz = jnp.where(j_pos <= i_pos, lz, 33)
+        idx[rows, 0:ke] = lz
+    h_hi = head.astype(BF16)
+    h_mid = (head - h_hi.astype(F32)).astype(BF16)
+    h_lo = (head - h_hi.astype(F32) - h_mid.astype(F32)).astype(BF16)
+    parts = jnp.concatenate([h_hi, h_mid, h_lo, jnp.zeros((13, D), BF16)], axis=0)
+    arrive(3)
+    hw = jnp.sum(nt(parts, w2_ref[...]), axis=0, keepdims=True)
     arrive(1)
     arrive(4)
     wait_bytes(recv.at[later], sems.at[3])
@@ -237,8 +268,6 @@
         slope[rows, :] = dh
         tok_ref[rows, :] = (held.astype(F32) + nn(hid, second_ref[...])).astype(BF16)
     wait_bytes(send.at[later], sems.at[2])
-    gain = gain_ref[...]
-    head = head_ref[...]
     scale = 1.0 / math.sqrt(HD)
     arrive(2)
     for s in range(0, LOOK, RB):
@@ -255,23 +284,6 @@
             y = p * sg
             proj[rows, cols] = y.astype(BF16)
             dsl[rows, cols] = (sg + y * (1.0 - sg)).astype(BF16)
-    lane = lax.broadcasted_iota(jnp.int32, (HEADS, 128), 1)
-    tab = jnp.zeros((HEADS, 128), F32)
-    for k in range(BUCKETS):
-        tab = tab + jnp.where(lane <= 31 - k, tb_ref[:, k : k + 1], 0.0)
-    tab = jnp.where(lane == 33, NEG, tab)
-    stamp_col = column(stamp_row_ref[...]).astype(jnp.int32)
-    for s in range(0, LOOK, RB):
-        rows = pl.ds(s, RB)
-        ke = keys_of(s)
-        now = jnp.concatenate([stamp_col[s : s + RB, :]] * (ke // 128), axis=1)
-        gap = now - stamp_row_ref[:, 0:ke]
-        lz = lax.clz(gap + 1)
-        if s < HIST:
-            i_pos = s + lax.broadcasted_iota(jnp.int32, (RB, ke), 0)
-            j_pos = lax.broadcasted_iota(jnp.int32, (RB, ke), 1)
-            lz = jnp.where(j_pos <= i_pos, lz, 33)
-        idx[rows, 0:ke] = lz
     for h in range(HEADS):
         hc = h * HD
         tab_h = jnp.broadcast_to(tab[h : h + 1, :], (RB, 128))
@@ -307,12 +319,6 @@
             ow = (y * (1.0 / HIST)).astype(BF16).astype(F32)
             own[h, s] = (ow, (sg + y * (1.0 - sg)) * (1.0 / HIST))
             att[rows, pl.ds(hc, HD)] += ow * v
-    h_hi = head.astype(BF16)
-    h_mid = (head - h_hi.astype(F32)).astype(BF16)
-    h_lo = (head - h_hi.astype(F32) - h_mid.astype(F32)).astype(BF16)
-    parts = jnp.concatenate([h_hi, h_mid, h_lo, jnp.zeros((13, D), BF16)], axis=0)
-    arrive(3)
-    hw = jnp.sum(nt(parts, w2_ref[...]), axis=0, keepdims=True)
     label_col = column(label_ref[...])
     loss = jnp.zeros((1, 1), F32)
     uvec = jnp.zeros((1, D), F32)
@@ -517,40 +523,36 @@
     u_start(1)
     row_grad = att[...].astype(BF16)
 
-    for t in range(ROWS // TILE):
-        base = t * TILE
-        rows = pl.ds(base, TILE)
-        pick = base + lax.broadcasted_iota(jnp.int32, (TILE, LOOK), 0) == slots
-        send[rows, :] = pack(nn(pick.astype(F32).astype(BF16), row_grad))
-
-        @pl.loop(*fresh(t))
+    for batch in range(OWNERS // BATCH):
+        base = batch * BATCH * SLOT
+        if base % TILE == 0:
+            rows = pl.ds(base, TILE)
+            pick = base + lax.broadcasted_iota(jnp.int32, (TILE, LOOK), 0) == slots
+            send[rows, :] = pack(nn(pick.astype(F32).astype(BF16), row_grad))
+        if batch == 0:
+            back_recv[0:SLOT, :] = send[0:SLOT, :]
+
+        @pl.loop(max(1, batch * BATCH), (batch + 1) * BATCH)
         def _(k):
             send_chunk(send, back_recv, k, (me + STEP * k) % OWNERS, sems.at[4], sems.at[5])
 
-        if t == 0:
-            finish(2, 0)
-            start(2, 1)
-    back_recv[0:SLOT, :] = send[0:SLOT, :]
-    for g in (0, 1):
-        finish(g, 1)
-        start(g, 2)
-    u_finish(1)
-    u_start(2)
-    finish(2, 1)
-    start(2, 2)
+        if batch in PLAN:
+            g, stage = PLAN[batch]
+            finish(g, stage)
+            start(g, stage + 1)
+            if g == 2 and stage > 0:
+                u_finish(stage)
+                if stage < 3:
+                    u_start(stage + 1)
+
     for s in range(0, D, 128):
         sub = (s + lax.broadcasted_iota(jnp.int32, (128, 128), 0)).astype(F32)
         for q in range(0, ROWS, 128):
             proj[pl.ds(s, 128), pl.ds(q, 128)] = (
                 (sub == idrow[0:1, q : q + 128]).astype(F32).astype(BF16)
             )
-    for stage in (2, 3):
-        for g in range(GROUPS):
-            finish(g, stage)
-            start(g, stage + 1)
-        u_finish(stage)
-        if stage == 2:
-            u_start(3)
+    finish(2, 4)
+    start(2, 5)
     wait_bytes(back_recv.at[later], sems.at[5])
     for s in range(0, ROWS, 256):
         rows = pl.ds(s, 256)
@@ -561,9 +563,6 @@
         att[rows, PACK:D] = nn(proj[rows, :], last[...])
     table_out = pltpu.make_async_copy(att.at[pl.ds(0, D), :], tablegrad_hbm, out_sems.at[3])
     table_out.start()
-    for g in range(GROUPS):
-        finish(g, 4)
-        start(g, 5)
     for g in range(GROUPS):
         finish(g, 5)
         own_half(g).wait()

time: 134 us -> 129 us (0.963)
  Pallas kernels: 132 us -> 127 us
    pallas_call x1, Pallas kernels: 126 us -> 121 us  [train_step(): pl.pallas_call(step_kernel, out_shape=(jax.ShapeDtypeStruct((D, D), F32),...]
where the time goes in v5:
time: 129 us
  Pallas kernels  127 us (98%)
  between operations  1.82 us (1%)
    pallas_call x1, Pallas kernels, train_step(): pl.pallas_call(step_kernel, out_shape=(jax.ShapeDtypeStruct((D, D), F32),...  121 us
    pallas_call x1, Pallas kernels, outputs(): pl.pallas_call(finish_kernel, grid=(D // n,), out_shape=(shape(D), shape(...  5.86 us

profile of v5, /device:TPU:1, one launch (start us, length us, event | category | flops | bytes accessed | tf_op | source)
XLA Modules:
  0.0 128.5 jit_solution(7349754402107502108)
XLA Ops:
  0.6 120.9 %step.1 = (f32[512,512]{1,0:T(8,128)}, bf16[6,512,512]{2,1,0:T(8,128)(2,1)}, f32[1,512]{1,0:T(1,128)}, f32[1,128]{1,0:T(1,128)}) custom-call(s32[1,768]{1,0:T(1,128)} %bitcast.7, s32[1,768]{1,0:T(1,128)} %row_ref.1, s32[1,768]{1,0:T(1,128)} %stamp_row_ref.1, s32[1,768]{1,0:T(1,128)} %label_ref.1, f32[1,512]{1,0:T(1,128)} %bitcast.8, f32[1,512]{1,0:T(1,128)} %bitcast.5, ...), custom_call_target="tpu_custom_call" | custom-call | flops 14000000000 | bytes 10485760 | tf_op jit(solution)/shard_map/step/pallas_call | solution.py:586
  121.5 0.0 copy-start
  121.5 5.9 %outputs.1 = (f32[512,512]{1,0:T(8,128)}, f32[512,512]{1,0:T(8,128)}, f32[512,512]{1,0:T(8,128)}, f32[512,2048]{1,0:T(8,128)}, f32[512,512]{1,0:T(8,128)}) custom-call(f32[512,512]{1,0:T(8,128)} %get-tuple-element.15.tablegrad_ref, bf16[6,512,512]{2,1,0:T(8,128)(2,1)} %get-tuple-element.16.sums_ref, f32[1,512]{1,0:T(1,128)} %get-tuple-element.17.usum_ref, ...), custom_call_target="tpu_custom_call" | custom-call | tf_op jit(solution)/shard_map/outputs/pallas_call | solution.py:668
  127.4 0.0 copy-done
Async XLA Ops:
  121.5 5.9 %copy-start = (f32[1,128]{1,0:T(1,128)S(1)}, f32[1,128]{1,0:T(1,128)}, u32[]{:S(2)}) copy-start(f32[1,128]{1,0:T(1,128)} %get-tuple-element.23) | copy-start | bytes 1540

commit v6 on v5

--- a/solution.py
+++ b/solution.py
@@ -138,10 +138,10 @@
     table_hbm, first_hbm, second_hbm, w1_hbm, w2_hbm,
     tablegrad_hbm, sums_hbm, usum_ref, loss_ref,
     sums_ref, table_ref, first_ref, second_ref, w1_ref, w2_ref,
-    ids_send, ids_recv, idq, idrow, send, recv, back_recv, last, rows_held, hidden, slope, tok_ref,
+    ids_send, ids_recv, idq, idrow, send, recv, back_recv, rows_held, hidden, slope, tok_ref,
     normed, proj, dsl, idx, wts, dwt, att, dp, de, dpre,
     terms, core_in, half, in1, part1, in2, u_held, u_in,
-    load_sems, out_sems, sems, send_sems, recv_sems, u_sems,
+    load_sems, out_sems, tile_sems, sems, send_sems, recv_sems, u_sems,
 ):
     user, item = place()
     me = user * 16 + item
@@ -217,7 +217,7 @@
         @pl.loop(*fresh(t))
         def _(k):
             target = (me - (STEP * k) % OWNERS + OWNERS) % OWNERS
-            send_chunk(send, recv, k, target, sems.at[2], sems.at[3])
+            send_chunk(send, recv, k, target, sems.at[2], tile_sems.at[0, t])
 
     recv[0:SLOT, :] = send[0:SLOT, :]
     idrow[...] = idq[...].T[0:8, :]
@@ -251,14 +251,27 @@
     hw = jnp.sum(nt(parts, w2_ref[...]), axis=0, keepdims=True)
     arrive(1)
     arrive(4)
-    wait_bytes(recv.at[later], sems.at[3])
-    for s in range(0, ROWS, 256):
-        rows = pl.ds(s, 256)
-        last[rows, :] = unpack_last(recv[rows, :])
-    for s in range(0, LOOK, 256):
-        rows = pl.ds(s, 256)
-        rows_held[rows, 0:PACK] = nn(dp[rows, :], recv[...]).astype(BF16)
-        rows_held[rows, PACK:D] = nn(dp[rows, :], last[...]).astype(BF16)
+    def tile_of(ref, t):
+        first = SLOT if t == 0 else 0
+        arrived = pl.ds(t * TILE + first, TILE - first)
+        wait_bytes(ref.at[arrived], tile_sems.at[0 if ref is recv else 1, t])
+        held = ref[t * TILE : (t + 1) * TILE, :]
+        return held, unpack_last(held)
+
+    def add_tile(ref, pick_ref, t, n):
+        held, end = tile_of(ref, t)
+        for s in range(0, n, 256):
+            rows = pl.ds(s, 256)
+            pick = pick_ref[rows, t * TILE : (t + 1) * TILE]
+            for cols, part in ((pl.ds(0, PACK), held), (pl.ds(PACK, 128), end)):
+                if t == 0:
+                    att[rows, cols] = nn(pick, part)
+                else:
+                    att[rows, cols] += nn(pick, part)
+
+    for t in range(ROWS // TILE):
+        add_tile(recv, dp, t, LOOK)
+    rows_held[...] = att[...].astype(BF16)
     for s in range(0, LOOK, 256):
         rows = pl.ds(s, 256)
         held = rows_held[rows, :]
@@ -521,7 +534,8 @@
         start(g, 1)
     u_finish(0)
     u_start(1)
-    row_grad = att[...].astype(BF16)
+    de[...] = att[...].astype(BF16)
+    row_grad = de[...]
 
     for batch in range(OWNERS // BATCH):
         base = batch * BATCH * SLOT
@@ -534,8 +548,17 @@
 
         @pl.loop(max(1, batch * BATCH), (batch + 1) * BATCH)
         def _(k):
-            send_chunk(send, back_recv, k, (me + STEP * k) % OWNERS, sems.at[4], sems.at[5])
-
+            send_chunk(send, back_recv, k, (me + STEP * k) % OWNERS, sems.at[4], tile_sems.at[1, base // TILE])
+
+        if batch == 1:
+            for s in range(0, D, 128):
+                sub = (s + lax.broadcasted_iota(jnp.int32, (128, 128), 0)).astype(F32)
+                for q in range(0, ROWS, 128):
+                    proj[pl.ds(s, 128), pl.ds(q, 128)] = (
+                        (sub == idrow[0:1, q : q + 128]).astype(F32).astype(BF16)
+                    )
+        if batch in (12, 13):
+            add_tile(back_recv, proj, batch - 12, D)
         if batch in PLAN:
             g, stage = PLAN[batch]
             finish(g, stage)
@@ -545,22 +568,10 @@
                 if stage < 3:
                     u_start(stage + 1)
 
-    for s in range(0, D, 128):
-        sub = (s + lax.broadcasted_iota(jnp.int32, (128, 128), 0)).astype(F32)
-        for q in range(0, ROWS, 128):
-            proj[pl.ds(s, 128), pl.ds(q, 128)] = (
-                (sub == idrow[0:1, q : q + 128]).astype(F32).astype(BF16)
-            )
     finish(2, 4)
     start(2, 5)
-    wait_bytes(back_recv.at[later], sems.at[5])
-    for s in range(0, ROWS, 256):
-        rows = pl.ds(s, 256)
-        last[rows, :] = unpack_last(back_recv[rows, :])
-    for s in range(0, D, 256):
-        rows = pl.ds(s, 256)
-        att[rows, 0:PACK] = nn(proj[rows, :], back_recv[...])
-        att[rows, PACK:D] = nn(proj[rows, :], last[...])
+    for t in (2, 3):
+        add_tile(back_recv, proj, t, D)
     table_out = pltpu.make_async_copy(att.at[pl.ds(0, D), :], tablegrad_hbm, out_sems.at[3])
     table_out.start()
     for g in range(GROUPS):
@@ -607,7 +618,6 @@
             pltpu.VMEM((ROWS, PACK), BF16),
             pltpu.VMEM((ROWS, PACK), BF16),
             pltpu.VMEM((ROWS, PACK), BF16),
-            pltpu.VMEM((ROWS, 128), BF16),
             pltpu.VMEM((LOOK, D), BF16),
             pltpu.VMEM((LOOK, D), BF16),
             pltpu.VMEM((LOOK, D), F32),
@@ -632,7 +642,8 @@
             pltpu.VMEM((4, 3, 1, D), F32),
             dma((5,)),
             dma((4,)),
-            dma((6,)),
+            dma((2, ROWS // TILE)),
+            dma((5,)),
             dma((GROUPS, 6, 15)),
             dma((GROUPS, 6, 15)),
             dma((2, 4, 3)),

time: 129 us -> 126 us (0.977)
  Pallas kernels: 127 us -> 124 us
    pallas_call x1, Pallas kernels: 121 us -> 118 us  [train_step(): pl.pallas_call(step_kernel, out_shape=(jax.ShapeDtypeStruct((D, D), F32),...]
where the time goes in v6:
time: 126 us
  Pallas kernels  124 us (98%)
  between operations  1.82 us (1%)
    pallas_call x1, Pallas kernels, train_step(): pl.pallas_call(step_kernel, out_shape=(jax.ShapeDtypeStruct((D, D), F32),...  118 us
    pallas_call x1, Pallas kernels, outputs(): pl.pallas_call(finish_kernel, grid=(D // n,), out_shape=(shape(D), shape(...  5.86 us

profile of v6, /device:TPU:1, one launch (start us, length us, event | category | flops | bytes accessed | tf_op | source)
XLA Modules:
  0.0 126.1 jit_solution(4260217934194991750)
XLA Ops:
  0.6 118.4 %step.1 = (f32[512,512]{1,0:T(8,128)}, bf16[6,512,512]{2,1,0:T(8,128)(2,1)}, f32[1,512]{1,0:T(1,128)}, f32[1,128]{1,0:T(1,128)}) custom-call(s32[1,768]{1,0:T(1,128)} %bitcast.7, s32[1,768]{1,0:T(1,128)} %row_ref.1, s32[1,768]{1,0:T(1,128)} %stamp_row_ref.1, s32[1,768]{1,0:T(1,128)} %label_ref.1, f32[1,512]{1,0:T(1,128)} %bitcast.8, f32[1,512]{1,0:T(1,128)} %bitcast.5, ...), custom_call_target="tpu_custom_call" | custom-call | flops 14000000000 | bytes 10485760 | tf_op jit(solution)/shard_map/step/pallas_call | solution.py:597
  119.0 0.0 copy-start
  119.1 5.9 %outputs.1 = (f32[512,512]{1,0:T(8,128)}, f32[512,512]{1,0:T(8,128)}, f32[512,512]{1,0:T(8,128)}, f32[512,2048]{1,0:T(8,128)}, f32[512,512]{1,0:T(8,128)}) custom-call(f32[512,512]{1,0:T(8,128)} %get-tuple-element.15.tablegrad_ref, bf16[6,512,512]{2,1,0:T(8,128)(2,1)} %get-tuple-element.16.sums_ref, f32[1,512]{1,0:T(1,128)} %get-tuple-element.17.usum_ref, ...), custom_call_target="tpu_custom_call" | custom-call | tf_op jit(solution)/shard_map/outputs/pallas_call | solution.py:679
  124.9 0.0 copy-done
Async XLA Ops:
  119.0 5.9 %copy-start = (f32[1,128]{1,0:T(1,128)S(1)}, f32[1,128]{1,0:T(1,128)}, u32[]{:S(2)}) copy-start(f32[1,128]{1,0:T(1,128)} %get-tuple-element.23) | copy-start | bytes 1540

commit v7 on v6

--- a/solution.py
+++ b/solution.py
@@ -128,8 +128,8 @@
 ORDER = ("xyz", "yzx", "zxy")
 BATCH = 8
 PLAN = {
-    0: (2, 0), 3: (0, 1), 4: (1, 1), 5: (2, 1), 6: (0, 2), 7: (1, 2), 8: (2, 2),
-    9: (0, 3), 10: (1, 3), 11: (2, 3), 14: (0, 4), 15: (1, 4),
+    0: (2, 0), 2: (0, 1), 3: (1, 1), 4: (2, 1), 5: (0, 2), 6: (1, 2), 7: (2, 2),
+    8: (0, 3), 9: (1, 3), 10: (2, 3), 13: (0, 4), 14: (1, 4),
 }
 
 

time: 126 us -> 128 us (1.016)
  Pallas kernels: 124 us -> 126 us
    pallas_call x1, Pallas kernels: 118 us -> 120 us  [train_step(): pl.pallas_call(step_kernel, out_shape=(jax.ShapeDtypeStruct((D, D), F32),...]
where the time goes in v7:
time: 128 us
  Pallas kernels  126 us (98%)
  between operations  1.82 us (1%)
    pallas_call x1, Pallas kernels, train_step(): pl.pallas_call(step_kernel, out_shape=(jax.ShapeDtypeStruct((D, D), F32),...  120 us
    pallas_call x1, Pallas kernels, outputs(): pl.pallas_call(finish_kernel, grid=(D // n,), out_shape=(shape(D), shape(...  5.86 us

profile of v7, /device:TPU:1, one launch (start us, length us, event | category | flops | bytes accessed | tf_op | source)
XLA Modules:
  0.0 128.0 jit_solution(16028380574825393577)
XLA Ops:
  0.6 120.3 %step.1 = (f32[512,512]{1,0:T(8,128)}, bf16[6,512,512]{2,1,0:T(8,128)(2,1)}, f32[1,512]{1,0:T(1,128)}, f32[1,128]{1,0:T(1,128)}) custom-call(s32[1,768]{1,0:T(1,128)} %bitcast.7, s32[1,768]{1,0:T(1,128)} %row_ref.1, s32[1,768]{1,0:T(1,128)} %stamp_row_ref.1, s32[1,768]{1,0:T(1,128)} %label_ref.1, f32[1,512]{1,0:T(1,128)} %bitcast.8, f32[1,512]{1,0:T(1,128)} %bitcast.5, ...), custom_call_target="tpu_custom_call" | custom-call | flops 14000000000 | bytes 10485760 | tf_op jit(solution)/shard_map/step/pallas_call | solution.py:597
  120.9 0.0 copy-start
  121.0 5.9 %outputs.1 = (f32[512,512]{1,0:T(8,128)}, f32[512,512]{1,0:T(8,128)}, f32[512,512]{1,0:T(8,128)}, f32[512,2048]{1,0:T(8,128)}, f32[512,512]{1,0:T(8,128)}) custom-call(f32[512,512]{1,0:T(8,128)} %get-tuple-element.15.tablegrad_ref, bf16[6,512,512]{2,1,0:T(8,128)(2,1)} %get-tuple-element.16.sums_ref, f32[1,512]{1,0:T(1,128)} %get-tuple-element.17.usum_ref, ...), custom_call_target="tpu_custom_call" | custom-call | tf_op jit(solution)/shard_map/outputs/pallas_call | solution.py:679
  126.8 0.0 copy-done
Async XLA Ops:
  120.9 5.9 %copy-start = (f32[1,128]{1,0:T(1,128)S(1)}, f32[1,128]{1,0:T(1,128)}, u32[]{:S(2)}) copy-start(f32[1,128]{1,0:T(1,128)} %get-tuple-element.23) | copy-start | bytes 1540
